TPU v7x, 32 devices: a whole 2x2x4 slice. The times are simulated.
32 devices in a mesh: gx: 4 (over z), gy: 8 (over y, x, core).
Axes of the slice: x: 2, y: 2, z: 4, core: 2. Of those that a mesh axis runs over, the one named last changes fastest.
Arguments:
- tokens: bfloat16 [64, 1024, 512], P(('gx', 'gy')), may hold values from -6 to 6
- segment_ids: int32 [64, 1024], P(('gx', 'gy')), may hold values from 0 to 5, never falling along the last dimension, each value on 1 to 512 neighbouring positions
- fill_lengths: int32 [64], P(('gx', 'gy')), may hold values from 256 to 1024
- joint_weight: bfloat16 [512, 1536], P(('gx', 'gy')), may hold values from -0.25 to 0.25
- joint_bias: bfloat16 [2, 512], P(None, ('gx', 'gy')), may hold values from -3 to 3
- mix_weight: bfloat16 [512, 512], P(('gx', 'gy')), may hold values from -1 to 1
- mix_bias: bfloat16 [512], P(('gx', 'gy')), may hold values from -3 to 3
- lift_weight: bfloat16 [512, 2048], P(('gx', 'gy')), may hold values from -0.25 to 0.25
- lift_bias: bfloat16 [2048], P(('gx', 'gy')), may hold values from -3 to 3
- drop_weight: bfloat16 [2048, 512], P(('gx', 'gy')), may hold values from -0.125 to 0.125
- drop_bias: bfloat16 [512], P(('gx', 'gy')), may hold values from -3 to 3
- cotangent: bfloat16 [64, 1024, 512], P(('gx', 'gy')), may hold values from -6 to 6
Outputs:
- layer_output: bfloat16 [64, 1024, 512], P(('gx', 'gy'))
- token_grad: float32 [64, 1024, 512], P(('gx', 'gy'))
- joint_weight_grad: float32 [512, 1536], P(('gx', 'gy'))
- joint_bias_grad: float32 [2, 512], P(None, ('gx', 'gy'))
- mix_weight_grad: float32 [512, 512], P(('gx', 'gy'))
- mix_bias_grad: float32 [512], P(('gx', 'gy'))
- lift_weight_grad: float32 [512, 2048], P(('gx', 'gy'))
- lift_bias_grad: float32 [2048], P(('gx', 'gy'))
- drop_weight_grad: float32 [2048, 512], P(('gx', 'gy'))
- drop_bias_grad: float32 [512], P(('gx', 'gy'))
Inputs may be any that keep to these rules, and one draw needn't show every extreme that they name: `segment_ids`: along each row the pair numbers never fall, and a pair holds 1 to 512 positions.
All inputs are finite; a program needn't handle non-finite values.
Results may differ from a plain program's by a relative error of at most 0.012.
The roundings to bfloat16 on the way count: a program that leaves them out, or rounds other values in their place, can miss the bound.
Values may be sent and summed in bfloat16 or wider, within the bound.
A program may use at most 192 MiB of HBM per device.

v0:
```python
import math

import jax
import jax.numpy as jnp
from jax import lax
from jax.sharding import PartitionSpec as P

HEADS = 8
HEAD = 64


def block_mask(seg_query, start, seg_row, fill_len, length):
    positions = jnp.arange(length, dtype=jnp.int32)
    row_ids = start + jnp.arange(seg_query.shape[0], dtype=jnp.int32)
    return (seg_query[:, None] == seg_row[None, :]) & (positions < fill_len)[None, :] | (
        row_ids[:, None] == positions[None, :]
    )


def block_scores(query_block, key_rows, allowed, score_scale):
    raw_scores = jnp.einsum(
        "qhd,khd->hqk", query_block, key_rows, preferred_element_type=jnp.float32
    )
    return jnp.where(allowed[None], raw_scores * score_scale, -1000000000.0)


def attend_row(row_item):
    row_parts, seg_row, fill_len = row_item
    length = row_parts.shape[0]
    block_size = min(512, length)
    block_count = length // block_size
    score_scale = 1.0 / math.sqrt(HEAD)
    key_rows = row_parts[:, 1]
    value_rows = row_parts[:, 2]
    query_blocks = row_parts[:, 0].reshape(block_count, block_size, HEADS, HEAD)
    seg_blocks = seg_row.reshape(block_count, block_size)
    starts = jnp.arange(block_count, dtype=jnp.int32) * block_size

    def one_block(block_item):
        query_block, seg_query, start = block_item
        allowed = block_mask(seg_query, start, seg_row, fill_len, length)
        scores = block_scores(query_block, key_rows, allowed, score_scale)
        row_max = jnp.max(scores, axis=-1, keepdims=True)
        exp_scores = jnp.exp(scores - row_max)
        row_total = jnp.sum(exp_scores, axis=-1, keepdims=True)
        weights = (exp_scores / row_total).astype(jnp.bfloat16)
        result = jnp.einsum("hqk,khd->qhd", weights, value_rows, preferred_element_type=jnp.float32)
        return (result, row_max + jnp.log(row_total))

    result, log_sums = lax.map(one_block, (query_blocks, seg_blocks, starts))
    return (result.reshape(length, HEADS * HEAD).astype(jnp.bfloat16), log_sums)


def attend_back(row_item):
    row_parts, seg_row, fill_len, log_sums, grad_out = row_item
    length = row_parts.shape[0]
    block_size = min(512, length)
    block_count = length // block_size
    score_scale = 1.0 / math.sqrt(HEAD)
    key_rows = row_parts[:, 1]
    value_rows = row_parts[:, 2]
    query_blocks = row_parts[:, 0].reshape(block_count, block_size, HEADS, HEAD)
    seg_blocks = seg_row.reshape(block_count, block_size)
    starts = jnp.arange(block_count, dtype=jnp.int32) * block_size
    grad_blocks = grad_out.reshape(block_count, block_size, HEADS, HEAD)
    zeros_init = jnp.zeros((length, HEADS, HEAD), jnp.float32)

    def one_block(running, block_item):
        grad_keys, grad_values = running
        query_block, seg_query, start, block_sum, grad_block = block_item
        allowed = block_mask(seg_query, start, seg_row, fill_len, length)
        scores = block_scores(query_block, key_rows, allowed, score_scale)
        weights = jnp.exp(scores - block_sum)
        weights_low = weights.astype(jnp.bfloat16)
        grad_values = grad_values + jnp.einsum(
            "hqk,qhd->khd", weights_low, grad_block, preferred_element_type=jnp.float32
        )
        grad_probs = jnp.einsum(
            "qhd,khd->hqk", grad_block, value_rows, preferred_element_type=jnp.float32
        )
        centre = jnp.sum(weights * grad_probs, axis=-1, keepdims=True)
        grad_scores = (weights * (grad_probs - centre)).astype(jnp.bfloat16)
        grad_query = (
            jnp.einsum("hqk,khd->qhd", grad_scores, key_rows, preferred_element_type=jnp.float32)
            * score_scale
        )
        grad_keys = (
            grad_keys
            + jnp.einsum(
                "hqk,qhd->khd", grad_scores, query_block, preferred_element_type=jnp.float32
            )
            * score_scale
        )
        return ((grad_keys, grad_values), grad_query)

    (grad_keys, grad_values), grad_queries = lax.scan(
        one_block,
        (zeros_init, zeros_init),
        (query_blocks, seg_blocks, starts, log_sums, grad_blocks),
    )
    return jnp.stack([grad_queries.reshape(length, HEADS, HEAD), grad_keys, grad_values], axis=1)


def body(
    tokens,
    segment_ids,
    fill_lengths,
    joint_weight,
    joint_bias,
    mix_weight,
    mix_bias,
    lift_weight,
    lift_bias,
    drop_weight,
    drop_bias,
    cotangent,
):
    rows_dev, length, model_width = tokens.shape
    attend_full = (
        lax.all_gather(joint_weight, ("gx", "gy"), axis=0, tiled=True),
        lax.all_gather(joint_bias, ("gx", "gy"), axis=1, tiled=True),
        lax.all_gather(mix_weight, ("gx", "gy"), axis=0, tiled=True),
        lax.all_gather(mix_bias, ("gx", "gy"), axis=0, tiled=True),
    )
    feed_full = (
        lax.all_gather(lift_weight, ("gx", "gy"), axis=0, tiled=True),
        lax.all_gather(lift_bias, ("gx", "gy"), axis=0, tiled=True),
        lax.all_gather(drop_weight, ("gx", "gy"), axis=0, tiled=True),
        lax.all_gather(drop_bias, ("gx", "gy"), axis=0, tiled=True),
    )
    joint_w, joint_b, mix_w, mix_b = attend_full
    lift_w, lift_b, drop_w, drop_b = feed_full
    flat_tokens = tokens.reshape(rows_dev * length, model_width)
    joint_shift = jnp.concatenate(
        [
            joint_b[0].astype(jnp.float32),
            jnp.zeros((model_width,), jnp.float32),
            joint_b[1].astype(jnp.float32),
        ]
    )
    joint_rows = (
        jnp.dot(flat_tokens, joint_w, preferred_element_type=jnp.float32) + joint_shift
    ).astype(jnp.bfloat16)
    row_parts = joint_rows.reshape(rows_dev, length, 3, HEADS, HEAD)
    context, log_sums = lax.map(attend_row, (row_parts, segment_ids, fill_lengths))
    context = context.reshape(rows_dev * length, model_width)
    middle = (
        flat_tokens.astype(jnp.float32)
        + jnp.dot(context, mix_w, preferred_element_type=jnp.float32)
        + mix_b.astype(jnp.float32)
    )
    middle_rows = middle.reshape(rows_dev, length, model_width)

    def feed_row(middle_row):
        hidden_in = middle_row.astype(jnp.bfloat16)
        lifted = jnp.dot(hidden_in, lift_w, preferred_element_type=jnp.float32) + lift_b.astype(
            jnp.float32
        )
        active = jax.nn.gelu(lifted).astype(jnp.bfloat16)
        return (
            middle_row
            + jnp.dot(active, drop_w, preferred_element_type=jnp.float32)
            + drop_b.astype(jnp.float32)
        )

    layer_output = lax.map(feed_row, middle_rows).astype(jnp.bfloat16)
    back_attend = (
        lax.all_gather(joint_weight, ("gx", "gy"), axis=0, tiled=True),
        lax.all_gather(joint_bias, ("gx", "gy"), axis=1, tiled=True),
        lax.all_gather(mix_weight, ("gx", "gy"), axis=0, tiled=True),
        lax.all_gather(mix_bias, ("gx", "gy"), axis=0, tiled=True),
    )
    back_feed = (
        lax.all_gather(lift_weight, ("gx", "gy"), axis=0, tiled=True),
        lax.all_gather(lift_bias, ("gx", "gy"), axis=0, tiled=True),
        lax.all_gather(drop_weight, ("gx", "gy"), axis=0, tiled=True),
        lax.all_gather(drop_bias, ("gx", "gy"), axis=0, tiled=True),
    )
    joint_w, joint_b, mix_w, mix_b = back_attend
    lift_w, lift_b, drop_w, drop_b = back_feed

    def feed_back(running, row_item):
        grad_lift, grad_lift_bias, grad_drop, grad_drop_bias = running
        middle_row, upstream = row_item
        hidden_in = middle_row.astype(jnp.bfloat16)
        lifted = jnp.dot(hidden_in, lift_w, preferred_element_type=jnp.float32) + lift_b.astype(
            jnp.float32
        )
        active, gelu_pull = jax.vjp(jax.nn.gelu, lifted)
        active_low = active.astype(jnp.bfloat16)
        grad_active = lax.dot_general(
            upstream, drop_w, (((1,), (1,)), ((), ())), preferred_element_type=jnp.float32
        )
        grad_drop = grad_drop + lax.dot_general(
            active_low, upstream, (((0,), (0,)), ((), ())), preferred_element_type=jnp.float32
        )
        grad_drop_bias = grad_drop_bias + jnp.sum(upstream.astype(jnp.float32), axis=0)
        grad_lifted = gelu_pull(grad_active)[0].astype(jnp.bfloat16)
        grad_lift = grad_lift + lax.dot_general(
            hidden_in, grad_lifted, (((0,), (0,)), ((), ())), preferred_element_type=jnp.float32
        )
        grad_lift_bias = grad_lift_bias + jnp.sum(grad_lifted.astype(jnp.float32), axis=0)
        grad_middle = upstream.astype(jnp.float32) + lax.dot_general(
            grad_lifted, lift_w, (((1,), (1,)), ((), ())), preferred_element_type=jnp.float32
        )
        return ((grad_lift, grad_lift_bias, grad_drop, grad_drop_bias), grad_middle)

    feed_init = (
        jnp.zeros(lift_w.shape, jnp.float32),
        jnp.zeros(lift_b.shape, jnp.float32),
        jnp.zeros(drop_w.shape, jnp.float32),
        jnp.zeros(drop_b.shape, jnp.float32),
    )
    feed_sums, grad_middle = lax.scan(feed_back, feed_init, (middle_rows, cotangent))
    feed_owned = (
        lax.psum_scatter(feed_sums[0], ("gx", "gy"), scatter_dimension=0, tiled=True),
        lax.psum_scatter(feed_sums[1], ("gx", "gy"), scatter_dimension=0, tiled=True),
        lax.psum_scatter(feed_sums[2], ("gx", "gy"), scatter_dimension=0, tiled=True),
        lax.psum_scatter(feed_sums[3], ("gx", "gy"), scatter_dimension=0, tiled=True),
    )
    grad_lift, grad_lift_bias, grad_drop, grad_drop_bias = feed_owned
    grad_middle = grad_middle.reshape(rows_dev * length, model_width)
    grad_branch = grad_middle.astype(jnp.bfloat16)
    grad_context = lax.dot_general(
        grad_branch, mix_w, (((1,), (1,)), ((), ())), preferred_element_type=jnp.float32
    ).astype(jnp.bfloat16)
    grad_mix = lax.dot_general(
        context, grad_branch, (((0,), (0,)), ((), ())), preferred_element_type=jnp.float32
    )
    grad_mix_bias = jnp.sum(grad_branch.astype(jnp.float32), axis=0)
    grad_parts = lax.map(
        attend_back,
        (
            row_parts,
            segment_ids,
            fill_lengths,
            log_sums,
            grad_context.reshape(rows_dev, length, HEADS, HEAD),
        ),
    )
    grad_joint = grad_parts.reshape(rows_dev * length, 3 * model_width).astype(jnp.bfloat16)
    grad_joint_weight = lax.dot_general(
        flat_tokens, grad_joint, (((0,), (0,)), ((), ())), preferred_element_type=jnp.float32
    )
    joint_sums = jnp.sum(grad_joint.astype(jnp.float32), axis=0)
    grad_joint_bias = jnp.stack([joint_sums[:model_width], joint_sums[2 * model_width :]])
    token_grad = grad_middle + lax.dot_general(
        grad_joint, joint_w, (((1,), (1,)), ((), ())), preferred_element_type=jnp.float32
    )
    attend_owned = (
        lax.psum_scatter(grad_joint_weight, ("gx", "gy"), scatter_dimension=0, tiled=True),
        lax.psum_scatter(grad_joint_bias, ("gx", "gy"), scatter_dimension=1, tiled=True),
        lax.psum_scatter(grad_mix, ("gx", "gy"), scatter_dimension=0, tiled=True),
        lax.psum_scatter(grad_mix_bias, ("gx", "gy"), scatter_dimension=0, tiled=True),
    )
    grad_joint_weight, grad_joint_bias, grad_mix, grad_mix_bias = attend_owned
    return (
        layer_output,
        token_grad.reshape(rows_dev, length, model_width),
        grad_joint_weight,
        grad_joint_bias,
        grad_mix,
        grad_mix_bias,
        grad_lift,
        grad_lift_bias,
        grad_drop,
        grad_drop_bias,
    )


def solution(mesh):
    in_specs = (
        P(("gx", "gy"), None, None),
        P(("gx", "gy"), None),
        P(("gx", "gy")),
        P(("gx", "gy"), None),
        P(None, ("gx", "gy")),
        P(("gx", "gy"), None),
        P(("gx", "gy")),
        P(("gx", "gy"), None),
        P(("gx", "gy")),
        P(("gx", "gy"), None),
        P(("gx", "gy")),
        P(("gx", "gy"), None, None),
    )
    out_specs = (
        P(("gx", "gy"), None, None),
        P(("gx", "gy"), None, None),
        P(("gx", "gy"), None),
        P(None, ("gx", "gy")),
        P(("gx", "gy"), None),
        P(("gx", "gy")),
        P(("gx", "gy"), None),
        P(("gx", "gy")),
        P(("gx", "gy"), None),
        P(("gx", "gy")),
    )
    return jax.shard_map(body, mesh=mesh, in_specs=in_specs, out_specs=out_specs, check_vma=False)
```

profile of v0, /device:TPU:0, one launch (start us, length us, event | category | flops | bytes accessed | tf_op | source)
XLA Modules:
  0.0 1284.0 jit_solution(1669774129701858011)
XLA Ops:
  12.1 42.1 %all-reduce.7 = (bf16[512]{0:T(512)(128)(2,1)S(1)}, bf16[2048]{0:T(1024)(128)(2,1)}, bf16[512]{0:T(512)(128)(2,1)}) all-reduce(bf16[512]{0:T(512)(128)(2,1)S(1)} %dynamic-update-slice, bf16[2048]{0:T(1024)(128)(2,1)S(1)} %dynamic-update-slice.1, bf16[512]{0:T(512)(128)(2,1)S(1)} %dynamic-update-slice.2), channel_id=1, replica_groups=mesh['gx'=4,'gy'=8] {'gx','gy'}, use_global_device_ids=true, to_apply=%add | all-reduce | flops 3072 | bytes 12288
  54.8 40.4 %all-gather = bf16[32,16,2]{1,2,0:T(2,128)(2,1)S(1)} all-gather(bf16[1,16,2]{1,2,0:T(2,128)(2,1)} %bitcast.311), channel_id=1, replica_groups=mesh['gx'=4,'gy'=8] {'gx','gy'}, dimensions={0}, use_global_device_ids=true | all-gather | bytes 2112 | tf_op jit(solution)/shard_map/all_gather | solution.py:121
  95.3 41.3 %all_gather.31 = bf16[512,512]{1,0:T(8,128)(2,1)} all-gather(bf16[16,512]{1,0:T(8,128)(2,1)} %param.29), channel_id=1, replica_groups=mesh['gx'=4,'gy'=8] {'gx','gy'}, dimensions={0}, use_global_device_ids=true | all-gather | bytes 540672 | tf_op jit(solution)/shard_map/all_gather | solution.py:122
  136.6 8.1 add_convert_fusion
  144.7 16.5 %reshape.287 = bf16[2,1024,3,8,64]{4,3,2,1,0:T(8,128)(2,1)} reshape(bf16[2048,1536]{1,0:T(8,128)(2,1)} %add_convert_fusion) | data formatting | bytes 12582912 | tf_op jit(solution)/shard_map/reshape | solution.py:144
  161.2 14.1 %copy.62 = bf16[2,1024,3,8,64]{1,4,3,2,0:T(8,128)(2,1)} copy(bf16[2,1024,3,8,64]{4,3,2,1,0:T(8,128)(2,1)} %reshape.287) | data formatting | bytes 12582912 | tf_op jit(solution)/shard_map/while | solution.py:145
  175.3 90.8 %while.89 = (s32[]{:T(128)}, bf16[2,1024,512]{1,2,0:T(8,128)(2,1)}, f32[2,2,8,512,1]{3,2,1,4,0:T(8,128)}, bf16[2,1024,3,8,64]{1,4,3,2,0:T(8,128)(2,1)}, s32[2,10...) while((s32[]{:T(128)}, bf16[2,1024,512]{1,2,0:T(8,128)(2,1)}, ...), condition=%wide.region_5.6_spmd.clone, body=%wide.region_0.5_spmd.sunk.clone | while | flops 1126168064 | bytes 91984344 | solution.py:145
  183.3 32.6 %while.88 = (s32[]{:T(128)}, bf16[2,512,8,64]{1,3,2,0:T(8,128)(2,1)}, f32[2,8,512,1]{2,1,3,0:T(8,128)S(1)}, s32[2,512]{1,0:T(2,128)S(1)}, s32[1024]{0:T(1024)S(1...) while((s32[]{:T(128)}, ...), condition=%wide.region_4.4_spmd, body=%wide.region_1.3_spmd.sunk | while | flops 1126168064 | bytes 68829424 | solution.py:50
  189.0 4.2 fusion.174
  193.3 5.4 fusion.175
  205.3 4.2 fusion.174
  209.6 5.4 fusion.175
  228.7 32.6 %while.88 = (s32[]{:T(128)}, bf16[2,512,8,64]{1,3,2,0:T(8,128)(2,1)}, f32[2,8,512,1]{2,1,3,0:T(8,128)S(1)}, s32[2,512]{1,0:T(2,128)S(1)}, s32[1024]{0:T(1024)S(1...) while((s32[]{:T(128)}, ...), condition=%wide.region_4.4_spmd, body=%wide.region_1.3_spmd.sunk | while | flops 1126168064 | bytes 68829424 | solution.py:50
  234.4 4.2 fusion.174
  238.7 5.4 fusion.175
  250.7 4.2 fusion.174
  255.0 5.4 fusion.175
  274.2 53.4 %while.93 = (s32[]{:T(128)}, f32[512,2048]{1,0:T(8,128)}, f32[2048]{0:T(1024)S(1)}, f32[2048,512]{1,0:T(8,128)}, f32[512]{0:T(512)S(1)}, /*index=5*/f32[2,1024,5...) while((s32[]{:T(128)}, f32[512,2048]{1,0:T(8,128)}, ...), condition=%wide.region_11.12_spmd.clone.clone, body=%wide.region_8.11_spmd.clone.sunk.clone | while | flops 10812920832 | bytes 195105200 | solution.py:214
  276.2 4.1 fusion.190
  280.3 5.6 select_add_fusion.14
  286.0 7.6 convert_reduce_fusion.8
  302.7 4.1 fusion.190
  306.8 5.6 select_add_fusion.14
  312.4 7.6 convert_reduce_fusion.8
  327.7 4.7 convert_reduce_fusion.3
  337.2 5.5 copy.66
  342.7 278.7 %while.92 = (s32[]{:T(128)}, bf16[2,1024,3,8,64]{1,4,3,2,0:T(8,128)(2,1)}, bf16[2,1024,3,8,64]{1,4,3,2,0:T(8,128)(2,1)}, s32[2,1024]{1,0:T(2,128)}, f32[2,2,8,51...) while((s32[]{:T(128)}, ...), condition=%wide.region_16.17_spmd.clone, body=%wide.region_12.16_spmd.sunk.clone | while | flops 2736780800 | bytes 239784592 | solution.py:231
  356.3 119.6 %while.91 = (s32[]{:T(128)}, f32[1024,8,64]{0,2,1:T(8,128)}, f32[1024,8,64]{0,2,1:T(8,128)}, bf16[2,512,8,64]{1,0,3,2:T(2,128)(2,1)}, bf16[2,512,8,64]{1,3,2,0:T...) while((s32[]{:T(128)}, f32[1024,8,64]{0,2,1:T(8,128)}, ...), condition=%wide.region_15.15_spmd.clone, body=%wide.region_13.14_spmd.clone.sunk | while | flops 2727343616 | bytes 206143856 | solution.py:96
  358.9 3.8 fusion.167
  362.6 11.1 multiply_reduce_fusion.2
  373.7 9.4 multiply_convert_fusion.8
  383.2 8.8 bitcast_add_fusion.7
  397.4 18.3 %dynamic_update_slice.55 = bf16[2,512,8,64]{1,0,3,2:T(2,128)(2,1)} dynamic-update-slice(bf16[2,512,8,64]{1,0,3,2:T(2,128)(2,1)} %get-tuple-element.1338, bf16[1,512,8,64]{1,0,3,2:T(2,128)(2,1)S(1)} %copy.89, s32[]{:T(128)S(6)} %copy.113, s32[]{:T(128)} %constant.157.clone.1..sunk.2..sunk, s32[]{:T(128)} %constant.157.clone.1..sunk.2..sunk, s32[]{:T(128)} %constant.157.clone.1..sunk.2..sunk) | dynamic-update-slice | bytes 1048580 | tf_op jit(solution)/shard_map/while/body/eval_jaxpr/while/body/jit(dynamic_update_index_in_dim)/dynamic_update_slice | solution.py:50
  418.4 3.8 fusion.167
  422.1 11.1 multiply_reduce_fusion.2
  433.2 9.4 multiply_convert_fusion.8
  442.7 9.4 bitcast_add_fusion.7
  457.5 18.3 %dynamic_update_slice.55 = bf16[2,512,8,64]{1,0,3,2:T(2,128)(2,1)} dynamic-update-slice(bf16[2,512,8,64]{1,0,3,2:T(2,128)(2,1)} %get-tuple-element.1338, bf16[1,512,8,64]{1,0,3,2:T(2,128)(2,1)S(1)} %copy.89, s32[]{:T(128)S(6)} %copy.113, s32[]{:T(128)} %constant.157.clone.1..sunk.2..sunk, s32[]{:T(128)} %constant.157.clone.1..sunk.2..sunk, s32[]{:T(128)} %constant.157.clone.1..sunk.2..sunk) | dynamic-update-slice | bytes 1048580 | tf_op jit(solution)/shard_map/while/body/eval_jaxpr/while/body/jit(dynamic_update_index_in_dim)/dynamic_update_slice | solution.py:50
  477.7 4.4 fusion.181
  495.4 119.6 %while.91 = (s32[]{:T(128)}, f32[1024,8,64]{0,2,1:T(8,128)}, f32[1024,8,64]{0,2,1:T(8,128)}, bf16[2,512,8,64]{1,0,3,2:T(2,128)(2,1)}, bf16[2,512,8,64]{1,3,2,0:T...) while((s32[]{:T(128)}, f32[1024,8,64]{0,2,1:T(8,128)}, ...), condition=%wide.region_15.15_spmd.clone, body=%wide.region_13.14_spmd.clone.sunk | while | flops 2727343616 | bytes 206143856 | solution.py:96
  498.0 3.8 fusion.167
  501.8 11.1 multiply_reduce_fusion.2
  512.9 9.4 multiply_convert_fusion.8
  522.3 8.8 bitcast_add_fusion.7
  536.6 18.3 %dynamic_update_slice.55 = bf16[2,512,8,64]{1,0,3,2:T(2,128)(2,1)} dynamic-update-slice(bf16[2,512,8,64]{1,0,3,2:T(2,128)(2,1)} %get-tuple-element.1338, bf16[1,512,8,64]{1,0,3,2:T(2,128)(2,1)S(1)} %copy.89, s32[]{:T(128)S(6)} %copy.113, s32[]{:T(128)} %constant.157.clone.1..sunk.2..sunk, s32[]{:T(128)} %constant.157.clone.1..sunk.2..sunk, s32[]{:T(128)} %constant.157.clone.1..sunk.2..sunk) | dynamic-update-slice | bytes 1048580 | tf_op jit(solution)/shard_map/while/body/eval_jaxpr/while/body/jit(dynamic_update_index_in_dim)/dynamic_update_slice | solution.py:50
  557.5 3.8 fusion.167
  561.3 11.1 multiply_reduce_fusion.2
  572.4 9.4 multiply_convert_fusion.8
  581.8 9.4 bitcast_add_fusion.7
  596.7 18.3 %dynamic_update_slice.55 = bf16[2,512,8,64]{1,0,3,2:T(2,128)(2,1)} dynamic-update-slice(bf16[2,512,8,64]{1,0,3,2:T(2,128)(2,1)} %get-tuple-element.1338, bf16[1,512,8,64]{1,0,3,2:T(2,128)(2,1)S(1)} %copy.89, s32[]{:T(128)S(6)} %copy.113, s32[]{:T(128)} %constant.157.clone.1..sunk.2..sunk, s32[]{:T(128)} %constant.157.clone.1..sunk.2..sunk, s32[]{:T(128)} %constant.157.clone.1..sunk.2..sunk) | dynamic-update-slice | bytes 1048580 | tf_op jit(solution)/shard_map/while/body/eval_jaxpr/while/body/jit(dynamic_update_index_in_dim)/dynamic_update_slice | solution.py:50
  616.8 4.4 fusion.181
  621.5 3.9 convert_reduce_fusion.2
  626.5 4.4 convolution_bitcast_fusion.1
  631.0 11.9 copy.67
  655.8 37.4 %all-reduce.6 = (f32[512]{0:T(512)S(1)}, f32[2048]{0:T(1024)S(1)}, f32[512]{0:T(512)S(1)}) all-reduce(f32[512]{0:T(512)S(1)} %copy-done.31, f32[2048]{0:T(1024)S(1)} %copy-done.26, f32[512]{0:T(512)S(1)} %copy-done.29), channel_id=5, replica_groups=mesh['gx'=4,'gy'=8] {'gx','gy'}, use_global_device_ids=true, to_apply=%region_22.23.clone | all-reduce | flops 3072 | bytes 24576
  695.0 10.0 bitcast_add_fusion.3
  705.0 17.1 %while.90 = (s32[]{:T(128)}, bf16[2,1024,512]{2,1,0:T(8,128)(2,1)S(1)}, f32[2,1024,512]{2,1,0:T(8,128)}, bf16[512,2048]{1,0:T(8,128)(2,1)}, bf16[2048]{0:T(1024)...) while((s32[]{:T(128)}, bf16[2,1024,512]{2,1,0:T(8,128)(2,1)S(1)}, ...), condition=%wide.region_7.8_spmd.clone, body=%wide.region_6.7_spmd.sunk.clone | while | flops 4317514240 | bytes 10512469 | solution.py:166
  705.0 8.5 bitcast_dynamic-update-slice_fusion.10
  713.6 8.5 bitcast_dynamic-update-slice_fusion.10
  722.1 35.4 %reduce-scatter.18.cloned.1.call-done = f32[16,2]{1,0:T(8,128)} async-done(((f32[512,2]{1,0:T(8,128)}), f32[16,2]{1,0:T(8,128)}) %reduce-scatter.18.cloned.1.call-update) | async-done | bytes 144
  758.9 132.1 %reduce-scatter.10.cloned.1.call-done = f32[16,512]{1,0:T(8,128)} async-done(((f32[512,512]{1,0:T(8,128)}), f32[16,512]{1,0:T(8,128)}) %reduce-scatter.10.cloned.1.call-update) | async-done | bytes 32784 | tf_op jit(solution)/shard_map/reduce_scatter | solution.py:253
  891.0 103.4 %reduce-scatter.16.cloned.1.call-done = f32[16,1536]{1,0:T(8,128)} async-done(((f32[512,1536]{1,0:T(8,128)}), f32[16,1536]{1,0:T(8,128)}) %reduce-scatter.16.cloned.1.call-update) | async-done | bytes 98320
  994.4 142.5 %reduce-scatter.12.cloned.1.call-done = f32[16,2048]{1,0:T(8,128)} async-done(((f32[512,2048]{1,0:T(8,128)}), f32[16,2048]{1,0:T(8,128)}) %reduce-scatter.12.cloned.1.call-update) | async-done | bytes 131088 | tf_op jit(solution)/shard_map/reduce_scatter | solution.py:216
  1137.0 139.8 %reduce-scatter.14.cloned.1.call-done = f32[64,512]{1,0:T(8,128)} async-done(((f32[2048,512]{1,0:T(8,128)}), f32[64,512]{1,0:T(8,128)}) %reduce-scatter.14.cloned.1.call-update) | async-done | bytes 131088 | tf_op jit(solution)/shard_map/reduce_scatter | solution.py:218
  (345 shorter events, 167.2 us)
Async XLA Ops:
  7.2 129.4 %all-gather.5.cloned.1.call-start = ((), (), s32[]{:S(2)}) async-start(), calls=%async_computation.5 | async-start | bytes 1622016 | tf_op jit(solution)/shard_map/all_gather | solution.py:120
  7.9 266.3 %all-gather.7.cloned.1.call-start = ((), (), s32[]{:S(2)}) async-start(), calls=%async_computation.6 | async-start | bytes 2162688 | tf_op jit(solution)/shard_map/all_gather | solution.py:126
  8.7 265.5 %all-gather.9.cloned.1.call-start = ((), (), s32[]{:S(2)}) async-start(), calls=%async_computation.7 | async-start | bytes 2162688 | tf_op jit(solution)/shard_map/all_gather | solution.py:128
  9.4 748.2 %reduce-scatter.18.cloned.1.call-start = ((), (), s32[]{:S(2)}) async-start(), calls=%async_computation.12 | async-start | bytes 270336
  189.0 4.3 copy-start.8
  189.0 4.3 copy-start.10
  205.3 4.3 copy-start.8
  205.3 4.3 copy-start.10
  234.4 4.3 copy-start.8
  234.4 4.3 copy-start.10
  250.7 4.3 copy-start.8
  250.7 4.3 copy-start.10
  266.1 2.9 copy-start.20
  266.1 2.9 copy-start.32
  276.2 4.1 copy-start.11
  276.2 4.1 copy-start.16
  280.3 5.6 copy-start.35
  285.9 7.6 copy-start.17
  286.0 7.7 copy-start.6
  293.6 3.1 copy-start.14
  293.6 3.1 copy-start.34
  302.6 4.1 copy-start.11
  302.6 4.1 copy-start.16
  306.8 5.6 copy-start.35
  312.4 7.6 copy-start.17
  312.4 7.7 copy-start.6
  320.1 3.1 copy-start.14
  320.1 3.1 copy-start.34
  327.7 6.0 copy-start.25
  327.7 6.0 copy-start.28
  327.7 4.7 copy-start.21
  373.7 9.4 copy-start.3
  383.2 8.8 copy-start
  383.2 8.8 copy-start.5
  392.0 2.7 copy-start.1
  392.0 2.7 copy-start.4
  396.5 19.2 %copy-start.2 = (f32[1024,8,64]{0,2,1:T(8,128)}, f32[1024,8,64]{0,2,1:T(8,128)S(1)}, u32[]{:S(2)}) copy-start(f32[1024,8,64]{0,2,1:T(8,128)S(1)} %bitcast_add_fusion.6) | copy-start | bytes 6291460 | tf_op jit(solution)/shard_map/while/body/eval_jaxpr/while
  433.2 9.4 copy-start.3
  442.7 9.4 copy-start
  442.7 9.4 copy-start.5
  452.1 2.7 copy-start.1
  452.1 2.7 copy-start.4
  456.6 19.2 %copy-start.2 = (f32[1024,8,64]{0,2,1:T(8,128)}, f32[1024,8,64]{0,2,1:T(8,128)S(1)}, u32[]{:S(2)}) copy-start(f32[1024,8,64]{0,2,1:T(8,128)S(1)} %bitcast_add_fusion.6) | copy-start | bytes 6291460 | tf_op jit(solution)/shard_map/while/body/eval_jaxpr/while
  512.9 9.4 copy-start.3
  522.3 8.8 copy-start
  522.3 8.8 copy-start.5
  531.2 2.7 copy-start.1
  531.2 2.7 copy-start.4
  535.7 19.2 %copy-start.2 = (f32[1024,8,64]{0,2,1:T(8,128)}, f32[1024,8,64]{0,2,1:T(8,128)S(1)}, u32[]{:S(2)}) copy-start(f32[1024,8,64]{0,2,1:T(8,128)S(1)} %bitcast_add_fusion.6) | copy-start | bytes 6291460 | tf_op jit(solution)/shard_map/while/body/eval_jaxpr/while
  572.4 9.4 copy-start.3
  581.8 9.4 copy-start
  581.8 9.4 copy-start.5
  591.3 2.7 copy-start.1
  591.3 2.7 copy-start.4
  595.8 19.2 %copy-start.2 = (f32[1024,8,64]{0,2,1:T(8,128)}, f32[1024,8,64]{0,2,1:T(8,128)S(1)}, u32[]{:S(2)}) copy-start(f32[1024,8,64]{0,2,1:T(8,128)S(1)} %bitcast_add_fusion.6) | copy-start | bytes 6291460 | tf_op jit(solution)/shard_map/while/body/eval_jaxpr/while
  621.4 5.0 copy-start.18
  626.4 264.6 %reduce-scatter.10.cloned.1.call-start = ((), (), s32[]{:S(2)}) async-start(), calls=%async_computation.8 | async-start | bytes 1081344 | tf_op jit(solution)/shard_map/reduce_scatter | solution.py:253
  630.9 363.5 %reduce-scatter.16.cloned.1.call-start = ((), (), s32[]{:S(2)}) async-start(), calls=%async_computation.11 | async-start | bytes 3244032
  642.9 5.3 copy-start.33
  654.1 482.9 %reduce-scatter.12.cloned.1.call-start = ((), (), s32[]{:S(2)}) async-start(), calls=%async_computation.9 | async-start | bytes 4325376 | tf_op jit(solution)/shard_map/reduce_scatter | solution.py:216
  654.9 621.8 %reduce-scatter.14.cloned.1.call-start = ((), (), s32[]{:S(2)}) async-start(), calls=%async_computation.10 | async-start | bytes 4325376 | tf_op jit(solution)/shard_map/reduce_scatter | solution.py:218
  695.0 10.0 copy-start.23
  695.0 10.0 copy-start.30
  722.1 554.6 %copy-start.19 = (bf16[2,1024,512]{2,1,0:T(8,128)(2,1)}, bf16[2,1024,512]{2,1,0:T(8,128)(2,1)S(1)}, u32[]{:S(2)}) copy-start(bf16[2,1024,512]{2,1,0:T(8,128)(2,1)S(1)} %get-tuple-element.381) | copy-start | bytes 6291460
  (16 other events, 27.1 us)
Sparse Core Ops, SparseCore 0:
  10.9 57.6 all-gather.4
  71.4 55.8 all-gather.6
  130.2 55.3 all-gather.8
  626.5 130.9 reduce-scatter.17
  760.3 130.6 reduce-scatter.9
  896.9 97.4 reduce-scatter.15
  997.3 139.6 reduce-scatter.11
  1139.8 136.8 reduce-scatter.13
where the time goes:
time: 1300 us; the launch traced here: 1280 us
  waiting for transfers between devices  557 us (43%)
  matrix products  240 us (18%)
  local copies, waits for them, and re-layouts  217 us (17%)
  blocking collectives  161 us (12%)
  other arithmetic  91.6 us (7%)
  between operations  15 us (1%)
    reduce_scatter x1, waiting for transfers between devices, body(): lax.psum_scatter(feed_sums[0], ('gx', 'gy'), scatter_dimension=0, tiled=T...  143 us
    unnamed x10, waiting for transfers between devices  142 us
    reduce_scatter x1, waiting for transfers between devices, body(): lax.psum_scatter(feed_sums[2], ('gx', 'gy'), scatter_dimension=0, tiled=T...  140 us
    reduce_scatter x1, waiting for transfers between devices, body(): lax.psum_scatter(grad_mix, ('gx', 'gy'), scatter_dimension=0, tiled=True)  132 us
    unnamed x2, blocking collectives  79.5 us
    dynamic_update_slice x8, local copies, waits for them, and re-layouts, attend_row(): result, log_sums = lax.map(one_block, (query_blocks, seg_blocks, starts))  76.9 us
    dot_general x8, matrix products, block_scores(): jnp.einsum('qhd,khd->hqk', query_block, key_rows, preferred_element_type=...  56.5 us
    all_gather x1, blocking collectives, body(): lax.all_gather(mix_weight, ('gx', 'gy'), axis=0, tiled=True)  41.3 us
  transfers between devices with their start and end apart: 8, of which 5 were waited for; matrix products, arithmetic and copies ran while one was open for 15% of the time, Pallas kernels for 0%

commit v1 on v0

v1 whole, which is shorter than its diff:
```python
import functools
import math

import jax
import jax.numpy as jnp
from jax import lax
from jax.experimental import pallas as pl
from jax.experimental.pallas import tpu as pltpu
from jax.sharding import PartitionSpec as P

BF = jnp.bfloat16
F32 = jnp.float32
NT = (((1,), (1,)), ((), ()))
NN = (((1,), (0,)), ((), ()))
NEG = -float(2**30)
C0 = math.sqrt(2.0 / math.pi)
C1 = 0.044715
CUT = 2
VMEM_LIMIT = 60 * 2**20


def mm(a, b, dims=NN):
    return lax.dot_general(a, b, dims, preferred_element_type=F32)


def split_heads(x):
    lane = lax.broadcasted_iota(jnp.int32, x.shape, 1)
    zero = jnp.zeros_like(x)
    return jnp.concatenate([jnp.where(lane < 64, x, zero), jnp.where(lane < 64, zero, x)], axis=0)


def diag_blocks(y):
    return jnp.concatenate([y[:64, :128], y[64:, 128:]], axis=0)


def window(starts_ref, fill_ref, row, t, length):
    first = t * 128
    last = first + 127
    fill = fill_ref[row]
    lo = jnp.int32(0)
    hi = jnp.int32(length)
    for v in range(1, 6):
        s = starts_ref[row, v]
        lo = jnp.where(s <= first, jnp.maximum(lo, s), lo)
        hi = jnp.where(s > last, jnp.minimum(hi, s), hi)
    hi = jnp.minimum(hi, fill)
    alone = lo >= fill
    hi = jnp.where(last >= fill, jnp.maximum(hi, last + 1), hi)
    lo = jnp.where(alone, first, lo)
    lo_b = lo // 128
    return lo_b, (hi + 127) // 128 - lo_b


def write_mask(mask_ref, segk_ref, seg_ref, fill, t, lo_b, n):
    segq = seg_ref[0, :, pl.ds(pl.multiple_of(t * 128, 128), 128)]
    segq = jnp.broadcast_to(segq, (128, 128))
    qi = t * 128 + lax.broadcasted_iota(jnp.int32, (128, 128), 1)
    ki0 = lax.broadcasted_iota(jnp.int32, (128, 128), 0)
    for c in range(n):
        off = pl.multiple_of((lo_b + c) * 128, 128)
        ki = ki0 + off
        ok = ((segk_ref[pl.ds(off, 128), :] == segq) & (ki < fill)) | (ki == qi)
        mask_ref[c * 128 : (c + 1) * 128, :] = jnp.where(ok, 0.0, NEG)


def spread_segments(seg_ref, segk_ref, length):
    for b in range(length // 128):
        row = seg_ref[0, :, b * 128 : (b + 1) * 128].astype(F32)
        segk_ref[b * 128 : (b + 1) * 128, :] = jnp.broadcast_to(row, (128, 128)).T.astype(jnp.int32)


def attend_kernel(
    starts_ref, fill_ref, seg_ref, qkv_ref, ctx_ref, lse_ref, vt_ref, segk_ref, mask_ref, s_ref, p_ref, *, length
):
    row = pl.program_id(0)
    fill = fill_ref[row]
    spread_segments(seg_ref, segk_ref, length)
    for b in range(length // 128):
        for p in range(4):
            v = qkv_ref[0, b * 128 : (b + 1) * 128, 1024 + p * 128 : 1024 + (p + 1) * 128]
            vt_ref[p * 128 : (p + 1) * 128, b * 128 : (b + 1) * 128] = v.T

    def tile(t, lo_b, n):
        tq = pl.ds(pl.multiple_of(t * 128, 128), 128)
        win = pl.ds(pl.multiple_of(lo_b * 128, 128), n * 128)
        cuts = [(c, min(CUT, n - c)) for c in range(0, n, CUT)]
        tops, sums = [], []
        for p in range(4):
            lanes = slice(p * 128, (p + 1) * 128)
            qbd = split_heads(qkv_ref[0, tq, lanes] * jnp.asarray(0.125, BF))
            top = None
            for c, w in cuts:
                rows = pl.ds(pl.multiple_of((lo_b + c) * 128, 128), w * 128)
                s = mm(qkv_ref[0, rows, 512 + p * 128 : 512 + (p + 1) * 128], qbd, NT)
                mask = mask_ref[c * 128 : (c + w) * 128, :]
                s = s + jnp.concatenate([mask, mask], axis=1)
                s_ref[p, c * 128 : (c + w) * 128, :] = s
                part = jnp.max(s.reshape(w * 16, 8, 256), axis=0)
                top = part if top is None else jnp.maximum(top, part)
            tops.append(jnp.max(top, axis=0, keepdims=True))
        for p in range(4):
            total = None
            for c, w in cuts:
                e = jnp.exp(s_ref[p, c * 128 : (c + w) * 128, :] - tops[p])
                p_ref[p, c * 128 : (c + w) * 128, :] = e.astype(BF)
                part = jnp.sum(e.reshape(w * 16, 8, 256), axis=0)
                total = part if total is None else total + part
            sums.append(jnp.sum(total, axis=0, keepdims=True))
        for p in range(4):
            o = mm(vt_ref[p * 128 : (p + 1) * 128, win], p_ref[p, : n * 128, :]) * (1.0 / sums[p])
            ctx_ref[0, tq, p * 128 : (p + 1) * 128] = diag_blocks(o).T.astype(BF)
            lse_ref[0, p, pl.ds(t, 1), :] = tops[p] + jnp.log(sums[p])

    @pl.loop(0, length // 128)
    def _(t):
        lo_b, n = window(starts_ref, fill_ref, row, t, length)
        for k in range(1, length // 128 + 1):

            @pl.when(n == k)
            def _(k=k):
                write_mask(mask_ref, segk_ref, seg_ref, fill, t, lo_b, k)
                tile(t, lo_b, k)


def attend(starts, fill, seg, qkv):
    rows, length, _ = qkv.shape
    blocks = length // 128
    return pl.pallas_call(
        functools.partial(attend_kernel, length=length),
        grid_spec=pltpu.PrefetchScalarGridSpec(
            num_scalar_prefetch=2,
            grid=(rows,),
            in_specs=[
                pl.BlockSpec((1, 1, length), lambda r, *_: (r, 0, 0)),
                pl.BlockSpec((1, length, 1536), lambda r, *_: (r, 0, 0)),
            ],
            out_specs=[
                pl.BlockSpec((1, length, 512), lambda r, *_: (r, 0, 0)),
                pl.BlockSpec((1, 4, blocks, 256), lambda r, *_: (r, 0, 0, 0)),
            ],
            scratch_shapes=[
                pltpu.VMEM((512, length), BF),
                pltpu.VMEM((length, 128), jnp.int32),
                pltpu.VMEM((length, 128), F32),
                pltpu.VMEM((4, length, 256), F32),
                pltpu.VMEM((4, length, 256), BF),
            ],
        ),
        out_shape=[
            jax.ShapeDtypeStruct((rows, length, 512), BF),
            jax.ShapeDtypeStruct((rows, 4, blocks, 256), F32),
        ],
        compiler_params=pltpu.CompilerParams(vmem_limit_bytes=VMEM_LIMIT),
        name="attend",
    )(starts, fill, seg, qkv)


def attend_back_kernel(
    starts_ref,
    fill_ref,
    seg_ref,
    qkv_ref,
    lse_ref,
    ctx_ref,
    do_ref,
    out_ref,
    kt_ref,
    segk_ref,
    mask_ref,
    dk_ref,
    dv_ref,
    p_ref,
    ds_ref,
    *,
    length,
):
    row = pl.program_id(0)
    fill = fill_ref[row]
    spread_segments(seg_ref, segk_ref, length)
    for b in range(length // 128):
        for p in range(4):
            k = qkv_ref[0, b * 128 : (b + 1) * 128, 512 + p * 128 : 512 + (p + 1) * 128]
            kt_ref[p * 128 : (p + 1) * 128, b * 128 : (b + 1) * 128] = k.T
    dk_ref[...] = jnp.zeros_like(dk_ref)
    dv_ref[...] = jnp.zeros_like(dv_ref)

    def tile(t, lo_b, n):
        tq = pl.ds(pl.multiple_of(t * 128, 128), 128)
        win = pl.ds(pl.multiple_of(lo_b * 128, 128), n * 128)
        ready = []
        for p in range(4):
            lanes = slice(p * 128, (p + 1) * 128)
            qbd = split_heads(qkv_ref[0, tq, lanes] * jnp.asarray(0.125, BF))
            do = do_ref[0, tq, lanes]
            prod = (do.astype(F32) * ctx_ref[0, tq, lanes].astype(F32)).T
            delta = jnp.concatenate(
                [jnp.sum(prod[:64], axis=0, keepdims=True), jnp.sum(prod[64:], axis=0, keepdims=True)], axis=1
            )
            ready.append((qbd, split_heads(do), delta, lse_ref[0, p, pl.ds(t, 1), :]))
        for c in range(0, n, CUT):
            w = min(CUT, n - c)
            rows = pl.ds(pl.multiple_of((lo_b + c) * 128, 128), w * 128)
            here = slice(c * 128, (c + w) * 128)
            for p in range(4):
                qbd, dobd, delta, lse = ready[p]
                s = mm(qkv_ref[0, rows, 512 + p * 128 : 512 + (p + 1) * 128], qbd, NT)
                dp = mm(qkv_ref[0, rows, 1024 + p * 128 : 1024 + (p + 1) * 128], dobd, NT)
                mask = mask_ref[here, :]
                e = jnp.exp(s + jnp.concatenate([mask, mask], axis=1) - lse)
                p_ref[p, here, :] = e.astype(BF)
                ds_ref[p, here, :] = (e * (dp - delta)).astype(BF)
            for p in range(4):
                qbd, dobd, _, _ = ready[p]
                lanes = slice(p * 128, (p + 1) * 128)
                dv_ref[rows, lanes] += mm(p_ref[p, here, :], dobd)
                dk_ref[rows, lanes] += mm(ds_ref[p, here, :], qbd)
        for p in range(4):
            lanes = slice(p * 128, (p + 1) * 128)
            dq = mm(kt_ref[lanes, win], ds_ref[p, : n * 128, :])
            out_ref[0, tq, lanes] = (diag_blocks(dq) * 0.125).T.astype(BF)

    @pl.loop(0, length // 128)
    def _(t):
        lo_b, n = window(starts_ref, fill_ref, row, t, length)
        for k in range(1, length // 128 + 1):

            @pl.when(n == k)
            def _(k=k):
                write_mask(mask_ref, segk_ref, seg_ref, fill, t, lo_b, k)
                tile(t, lo_b, k)

    out_ref[0, :, 512:1024] = dk_ref[...].astype(BF)
    out_ref[0, :, 1024:1536] = dv_ref[...].astype(BF)


def attend_back(starts, fill, seg, qkv, lse, ctx, do):
    rows, length, _ = qkv.shape
    blocks = length // 128
    return pl.pallas_call(
        functools.partial(attend_back_kernel, length=length),
        grid_spec=pltpu.PrefetchScalarGridSpec(
            num_scalar_prefetch=2,
            grid=(rows,),
            in_specs=[
                pl.BlockSpec((1, 1, length), lambda r, *_: (r, 0, 0)),
                pl.BlockSpec((1, length, 1536), lambda r, *_: (r, 0, 0)),
                pl.BlockSpec((1, 4, blocks, 256), lambda r, *_: (r, 0, 0, 0)),
                pl.BlockSpec((1, length, 512), lambda r, *_: (r, 0, 0)),
                pl.BlockSpec((1, length, 512), lambda r, *_: (r, 0, 0)),
            ],
            out_specs=pl.BlockSpec((1, length, 1536), lambda r, *_: (r, 0, 0)),
            scratch_shapes=[
                pltpu.VMEM((512, length), BF),
                pltpu.VMEM((length, 128), jnp.int32),
                pltpu.VMEM((length, 128), F32),
                pltpu.VMEM((length, 512), F32),
                pltpu.VMEM((length, 512), F32),
                pltpu.VMEM((4, length, 256), BF),
                pltpu.VMEM((4, length, 256), BF),
            ],
        ),
        out_shape=jax.ShapeDtypeStruct((rows, length, 1536), BF),
        compiler_params=pltpu.CompilerParams(vmem_limit_bytes=VMEM_LIMIT),
        name="attend_back",
    )(starts, fill, seg, qkv, lse, ctx, do)


def gelu_pair(x, grad):
    x2 = x * x
    h = 0.5 + 0.5 * jnp.tanh(x * (C0 + (C0 * C1) * x2))
    act = x * h
    slope = h + act * (1.0 - h) * (2.0 * C0 + (6.0 * C0 * C1) * x2)
    return act.astype(BF), (grad * slope).astype(BF)


def feed_kernel(
    tok_ref,
    ctx_ref,
    cot_ref,
    mix_ref,
    lift_ref,
    drop_ref,
    bias_ref,
    out_ref,
    gmid_ref,
    gctx_ref,
    glift_ref,
    gdrop_ref,
    gmix_ref,
    gbias_ref,
    hid_ref,
    hidt_ref,
    cott_ref,
    acc_ref,
    act_ref,
    gl_ref,
    *,
    tb,
):
    tokens, width = tok_ref.shape
    nf = lift_ref.shape[0]
    nb = tokens // tb
    ones = jnp.ones((16, tb), BF)

    @pl.loop(0, nb)
    def _(b):
        rows = pl.ds(pl.multiple_of(b * tb, tb), tb)
        mid = tok_ref[rows, :].astype(F32) + mm(ctx_ref[rows, :], mix_ref[...]) + bias_ref[5:6, :]
        acc_ref[rows, :] = mid + bias_ref[4:5, :]
        h = mid.astype(BF)
        hid_ref[rows, :] = h
        hidt_ref[0:width, rows] = h.T
        hidt_ref[width : width + 16, rows] = ones
        c = cot_ref[rows, :]
        cott_ref[:, rows] = c.T
        gmid_ref[rows, :] = c.astype(F32)

    def stage1(f, b):
        rows = pl.ds(b * tb, tb)
        for n in range(0, 512, 256):
            x = mm(hid_ref[rows, :], lift_ref[f, :, n : n + 256]) + bias_ref[pl.ds(f, 1), n : n + 256]
            grad = mm(cot_ref[rows, :], drop_ref[f, n : n + 256, :], NT)
            a, g = gelu_pair(x, grad)
            act_ref[b, :, n : n + 256] = a
            gl_ref[b, :, n : n + 256] = g

    def stage2(f, b):
        rows = pl.ds(b * tb, tb)
        act = act_ref[b]
        gl = gl_ref[b]
        acc_ref[rows, :] += mm(act, drop_ref[f])
        gmid_ref[rows, :] += mm(gl, lift_ref[f], NT)
        gd = mm(cott_ref[:, rows], act)
        gf = mm(hidt_ref[:, rows], gl)
        if b == 0:
            gdrop_ref[f] = gd
            glift_ref[f] = gf
        else:
            gdrop_ref[f] += gd
            glift_ref[f] += gf

    @pl.loop(0, nf)
    def _(f):
        stage1(f, 0)
        for b in range(1, nb):
            stage1(f, b)
            stage2(f, b - 1)
        stage2(f, nb - 1)

    gmix_ref[...] = jnp.zeros_like(gmix_ref)
    gbias_ref[...] = jnp.zeros_like(gbias_ref)

    @pl.loop(0, nb)
    def _(b):
        rows = pl.ds(pl.multiple_of(b * tb, tb), tb)
        out_ref[rows, :] = acc_ref[rows, :].astype(BF)
        gb = gmid_ref[rows, :].astype(BF)
        gctx_ref[rows, :] = mm(gb, mix_ref[...], NT).astype(BF)
        gmix_ref[...] += mm(ctx_ref[rows, :].T, gb)
        gbias_ref[5:6, :] += mm(ones, gb)[0:1]
        gbias_ref[4:5, :] += mm(ones, cot_ref[rows, :])[0:1]

    for f in range(nf):
        gbias_ref[f : f + 1, :] = glift_ref[f, width : width + 1, :]


def feed(tok, ctx, cot, mix, lift, drop, bias):
    tokens, width = tok.shape
    nf = lift.shape[0]
    tb = 512
    vmem = pl.BlockSpec(memory_space=pltpu.VMEM)
    return pl.pallas_call(
        functools.partial(feed_kernel, tb=tb),
        in_specs=[vmem] * 7,
        out_specs=[vmem] * 7,
        out_shape=[
            jax.ShapeDtypeStruct((tokens, width), BF),
            jax.ShapeDtypeStruct((tokens, width), F32),
            jax.ShapeDtypeStruct((tokens, width), BF),
            jax.ShapeDtypeStruct((nf, width + 16, 512), F32),
            jax.ShapeDtypeStruct((nf, width, 512), F32),
            jax.ShapeDtypeStruct((width, width), F32),
            jax.ShapeDtypeStruct((8, 512), F32),
        ],
        scratch_shapes=[
            pltpu.VMEM((tokens, width), BF),
            pltpu.VMEM((width + 16, tokens), BF),
            pltpu.VMEM((width, tokens), BF),
            pltpu.VMEM((tokens, width), F32),
            pltpu.VMEM((tokens // tb, tb, 512), BF),
            pltpu.VMEM((tokens // tb, tb, 512), BF),
        ],
        compiler_params=pltpu.CompilerParams(vmem_limit_bytes=VMEM_LIMIT),
        name="feed",
    )(tok, ctx, cot, mix, lift, drop, bias)


BOTH = ("gx", "gy")


def body(
    tokens,
    segment_ids,
    fill_lengths,
    joint_weight,
    joint_bias,
    mix_weight,
    mix_bias,
    lift_weight,
    lift_bias,
    drop_weight,
    drop_bias,
    cotangent,
):
    rows, length, width = tokens.shape
    n_tok = rows * length
    tok = tokens.reshape(n_tok, width)
    cot = cotangent.reshape(n_tok, width)
    seg = segment_ids.reshape(rows, 1, length)
    starts = jnp.sum(
        segment_ids[:, None, :] < jnp.arange(8, dtype=jnp.int32)[None, :, None], axis=-1, dtype=jnp.int32
    )

    joint_w = lax.all_gather(joint_weight, BOTH, axis=0, tiled=True)
    mix_w = lax.all_gather(mix_weight, BOTH, axis=0, tiled=True)
    lift_w = lax.all_gather(lift_weight, BOTH, axis=0, tiled=True)
    drop_w = lax.all_gather(drop_weight, BOTH, axis=0, tiled=True)
    own_bias = jnp.concatenate([joint_bias.reshape(-1), mix_bias, lift_bias, drop_bias])
    sizes = [joint_bias.shape[1], joint_bias.shape[1], mix_bias.size, lift_bias.size, drop_bias.size]
    all_bias = lax.all_gather(own_bias, BOTH, axis=0)
    parts, at = [], 0
    for size in sizes:
        parts.append(all_bias[:, at : at + size].reshape(-1).astype(F32))
        at += size
    bq, bv, bm, bl, bd = parts
    nf = bl.size // 512
    bias = jnp.concatenate(
        [jnp.concatenate([bl.reshape(nf, 512), jnp.zeros((4 - nf, 512), F32)]), bd[None], bm[None], bq[None], bv[None]]
    )

    shift = jnp.concatenate([bq, jnp.zeros_like(bq), bv])
    qkv = (mm(tok, joint_w) + shift).astype(BF)
    qkv3 = qkv.reshape(rows, length, 3 * width)
    ctx, lse = attend(starts, fill_lengths, seg, qkv3)
    lift_units = lift_w.reshape(width, nf, 512).transpose(1, 0, 2)
    out, gmid, gctx, glift, gdrop, gmix, gbias = feed(
        tok, ctx.reshape(n_tok, width), cot, mix_w, lift_units, drop_w.reshape(nf, 512, width), bias
    )
    gjoint = attend_back(
        starts, fill_lengths, seg, qkv3, lse, ctx, gctx.reshape(rows, length, width)
    ).reshape(n_tok, 3 * width)
    gjoint_w = lax.dot_general(tok, gjoint, (((0,), (0,)), ((), ())), preferred_element_type=F32)
    sums = jnp.sum(gjoint.astype(F32), axis=0)
    token_grad = gmid + mm(gjoint, joint_w, NT)

    glift_w = glift[:, :width].transpose(1, 0, 2).reshape(width, nf * 512)
    gdrop_w = gdrop.transpose(0, 2, 1).reshape(nf * 512, width)
    scatter = functools.partial(lax.psum_scatter, axis_name=BOTH, scatter_dimension=0, tiled=True)
    n_dev = all_bias.shape[0]
    packed = jnp.concatenate(
        [
            g.reshape(n_dev, -1)
            for g in (sums[:width], sums[2 * width :], gbias[5], gbias[:nf].reshape(-1), gbias[4])
        ],
        axis=1,
    )
    own = scatter(packed)[0]
    cuts, at = [], 0
    for size in sizes:
        cuts.append(own[at : at + size])
        at += size
    return (
        out.reshape(rows, length, width),
        token_grad.reshape(rows, length, width),
        scatter(gjoint_w),
        jnp.stack([cuts[0], cuts[1]]),
        scatter(gmix),
        cuts[2],
        scatter(glift_w),
        cuts[3],
        scatter(gdrop_w),
        cuts[4],
    )


def solution(mesh):
    wide = P(BOTH, None, None)
    rows = P(BOTH, None)
    flat = P(BOTH)
    bias = P(None, BOTH)
    in_specs = (wide, rows, flat, rows, bias, rows, flat, rows, flat, rows, flat, wide)
    out_specs = (wide, wide, rows, bias, rows, flat, rows, flat, rows, flat)
    return jax.shard_map(body, mesh=mesh, in_specs=in_specs, out_specs=out_specs, check_vma=False)
```

time: 1300 us -> 762 us (0.59)
  matrix products: 240 us -> 22.8 us
  local copies, waits for them, and re-layouts: 217 us -> 32.7 us
  waiting for transfers between devices: 557 us -> 460 us
  Pallas kernels: 0 us -> 90.6 us
  other arithmetic: 91.6 us -> 7.29 us
  blocking collectives: 161 us -> 129 us
    reduce_scatter x3 -> x2, waiting for transfers between devices: 414 us -> 158 us  [the longest x1 140 us: body(): scatter(gdrop_w)]
    dot_general x46 -> x3, matrix products: 240 us -> 22.8 us  [the longest x2 16.6 us: mm(): return lax.dot_general(a, b, dims, preferred_element_type=F32)]
    unnamed x10 -> x9, waiting for transfers between devices: 142 us -> 249 us
    pallas_call x0 -> x3, Pallas kernels: none -> 90.6 us  [the longest x1 43.8 us: feed(): pl.pallas_call(functools.partial(feed_kernel, tb=tb), in_specs=[vmem] * 7...]
    dynamic_update_slice x12 -> x0, local copies, waits for them, and re-layouts: 80.2 us -> none  [the longest x8 76.9 us: attend_row(): result, log_sums = lax.map(one_block, (query_blocks, seg_blocks, starts))]
    all_gather x3, waiting for transfers between devices: 0.06 us -> 52.7 us  [the longest x1 52.7 us: body(): drop_w = lax.all_gather(drop_weight, BOTH, axis=0, tiled=True)]
    convert_element_type x12 -> x0, other arithmetic: 38.4 us -> none  [the longest x4 37.7 us: one_block(): grad_scores = (weights * (grad_probs - centre)).astype(jnp.bfloat16)]
    while x117 -> x0, local copies, waits for them, and re-layouts: 35.8 us -> none  [the longest x2 17 us: body(): lax.map(attend_row, (row_parts, segment_ids, fill_lengths))]
  transfers between devices with their start and end apart: 8 -> 7, of which waited for: 5 -> 5; matrix products, arithmetic and copies ran while one was open for 15% -> 8% of each run, Pallas kernels for 0% -> 6%
where the time goes in v1:
time: 762 us; the launch traced here: 757 us
  waiting for transfers between devices  460 us (60%)
  blocking collectives  129 us (17%)
  Pallas kernels  90.6 us (12%)
  local copies, waits for them, and re-layouts  32.7 us (4%)
  matrix products  22.8 us (3%)
  between operations  14.5 us (2%)
    unnamed x9, waiting for transfers between devices  249 us
    reduce_scatter x1, waiting for transfers between devices, body(): scatter(gdrop_w)  140 us
    all_gather x1, waiting for transfers between devices, body(): drop_w = lax.all_gather(drop_weight, BOTH, axis=0, tiled=True)  52.7 us
    unnamed x1, blocking collectives  44.8 us
    pallas_call x1, Pallas kernels, feed(): pl.pallas_call(functools.partial(feed_kernel, tb=tb), in_specs=[vmem] * 7...  43.8 us
    all_gather x1, blocking collectives, body(): all_bias = lax.all_gather(own_bias, BOTH, axis=0)  43 us
    all_gather x1, blocking collectives, body(): mix_w = lax.all_gather(mix_weight, BOTH, axis=0, tiled=True)  41 us
    pallas_call x1, Pallas kernels, attend_back(): pl.pallas_call(functools.partial(attend_back_kernel, length=length), grid...  26.4 us
  transfers between devices with their start and end apart: 7, of which 5 were waited for; matrix products, arithmetic and copies ran while one was open for 8% of the time, Pallas kernels for 6%

profile of v1, /device:TPU:0, one launch (start us, length us, event | category | flops | bytes accessed | tf_op | source)
XLA Modules:
  0.0 757.2 jit_solution(521896650396545250)
XLA Ops:
  7.2 0.0 all-gather.6.cloned.1.call-start
  7.2 0.7 all-gather.6.cloned.1.call-update
  7.9 0.0 all-gather.8.cloned.1.call-start
  8.0 0.7 all-gather.8.cloned.1.call-update
  8.7 0.0 all-gather.10.cloned.1.call-start
  8.7 0.7 all-gather.10.cloned.1.call-update
  9.4 0.0 reduce-scatter.9.cloned.1.call-start
  9.4 0.7 reshape.153
  10.2 0.8 maximum_bitcast_fusion
  10.9 43.0 %all-gather.1 = bf16[32,1,128]{2,1,0:T(2,128)(2,1)S(1)} all-gather(bf16[1,1,128]{2,1,0:T(2,128)(2,1)S(1)} %maximum_bitcast_fusion), channel_id=2, replica_groups=mesh['gx'=4,'gy'=8] {'gx','gy'}, dimensions={0}, use_global_device_ids=true | all-gather | bytes 8448 | tf_op jit(solution)/shard_map/all_gather | solution.py:430
  54.0 0.1 slice.96
  54.0 0.1 fusion.1
  54.1 0.1 convert_element_type.76
  54.2 0.1 convert_element_type.77
  54.3 0.1 convert_element_type.78
  54.4 0.1 convert_element_type.79
  54.5 0.1 convert_element_type.75
  54.6 0.6 concatenate.17.bias_ref
  55.2 0.1 reshape.167
  55.3 0.1 reshape.168
  55.4 1.3 broadcast_in_dim.4.seg_ref
  56.7 1.4 convert_reduce_fusion.1.starts_ref
  58.1 41.0 %all_gather.21.mix_ref = bf16[512,512]{1,0:T(8,128)(2,1)} all-gather(bf16[16,512]{1,0:T(8,128)(2,1)} %param.17), channel_id=1, replica_groups=mesh['gx'=4,'gy'=8] {'gx','gy'}, dimensions={0}, use_global_device_ids=true | all-gather | bytes 540672 | tf_op jit(solution)/shard_map/all_gather | solution.py:425
  99.1 0.0 all-gather.6.cloned.1.call-done
  99.1 8.1 %add_convert_fusion = bf16[2048,1536]{1,0:T(8,128)(2,1)} fusion(bf16[2048,512]{1,0:T(8,128)(2,1)} %bitcast.50, bf16[512,1536]{1,0:T(8,128)(2,1)} %all-gather.6.cloned.1.call-done, f32[1536]{0:T(1024)S(1)} %pad_maximum_fusion), kind=kOutput, calls=%fused_computation.1 | convolution fusion | flops 3227516928 | bytes 9967616 | tf_op jit(solution)/shard_map/dot_general | solution.py:23
  107.3 20.4 %attend.1 = (bf16[2,1024,512]{2,1,0:T(8,128)(2,1)}, f32[2,4,8,256]{3,2,1,0:T(8,128)}) custom-call(s32[2,8]{1,0:T(2,128)} %convert_reduce_fusion.1.starts_ref, s32[2]{0:T(128)} %fill_ref.3, s32[2,1,1024]{2,1,0:T(1,128)} %broadcast_in_dim.4.seg_ref, bf16[2,1024,1536]{2,1,0:T(8,128)(2,1)} %bitcast.40), custom_call_target="tpu_custom_call" | custom-call | tf_op jit(solution)/shard_map/attend/pallas_call | solution.py:128
  127.7 2.9 copy.38
  130.6 2.4 copy.39
  133.0 52.7 %all-gather.10.cloned.1.call-done = bf16[2048,512]{1,0:T(8,128)(2,1)} async-done(((bf16[64,512]{1,0:T(8,128)(2,1)}), bf16[2048,512]{1,0:T(8,128)(2,1)}) %all-gather.10.cloned.1.call-update) | async-done | bytes 2097168 | tf_op jit(solution)/shard_map/all_gather | solution.py:427
  185.7 43.8 %feed.1 = (bf16[2048,512]{1,0:T(8,128)(2,1)}, f32[2048,512]{1,0:T(8,128)}, bf16[2048,512]{1,0:T(8,128)(2,1)}, f32[4,528,512]{2,1,0:T(8,128)}, f32[4,512,512]{2,1...) custom-call(bf16[2048,512]{1,0:T(8,128)(2,1)} %bitcast.51, bf16[2048,512]{1,0:T(8,128)(2,1)} %bitcast.44, ...), custom_call_target="tpu_custom_call" | custom-call | tf_op jit(solution)/shard_map/feed/pallas_call | solution.py:372
  229.4 0.0 reduce-scatter.9.cloned.1.call-update
  229.5 0.0 reduce-scatter.13.cloned.1.call-start
  229.5 26.4 %attend_back.1 = bf16[2,1024,1536]{2,1,0:T(8,128)(2,1)} custom-call(s32[2,8]{1,0:T(2,128)} %convert_reduce_fusion.1.starts_ref, s32[2]{0:T(128)} %fill_ref.3, s32[2,1,1024]{2,1,0:T(1,128)} %broadcast_in_dim.4.seg_ref, bf16[2,1024,1536]{2,1,0:T(8,128)(2,1)} %bitcast.41, f32[2,4,8,256]{3,2,1,0:T(8,128)} %get-tuple-element.22.lse_ref, ...), custom_call_target="tpu_custom_call" | custom-call | tf_op jit(solution)/shard_map/attend_back/pallas_call | solution.py:239
  255.9 6.2 convolution_bitcast_fusion
  262.2 2.4 copy.46
  264.5 0.0 reduce-scatter.13.cloned.1.call-update
  264.6 0.0 reduce-scatter.15.cloned.1.call-start
  264.6 4.7 slice_bitcast_fusion
  269.3 5.2 copy.41
  274.5 5.5 copy.48
  280.0 0.0 reduce-scatter.15.cloned.1.call-update
  280.0 0.0 reduce-scatter.11.cloned.1.call-start
  280.0 5.2 copy.42
  285.3 0.0 reduce-scatter.11.cloned.1.call-update
  285.3 0.0 copy-start
  285.3 0.0 copy-start.1
  285.3 3.8 convert_reduce_fusion
  289.2 0.1 reshape.163
  289.3 0.1 reshape.164
  289.3 0.0 copy-done
  289.4 0.1 reshape_squeeze.6
  289.4 0.1 reshape_squeeze.7
  289.5 0.1 reshape_reshape.3
  289.6 0.1 concatenate.18
  289.7 44.8 %all-reduce = f32[32,128]{1,0:T(8,128)S(1)} all-reduce(f32[32,128]{1,0:T(8,128)S(1)} %concatenate.18), channel_id=4, replica_groups=mesh['gx'=4,'gy'=8] {'gx','gy'}, use_global_device_ids=true, to_apply=%region_3.0.clone | all-reduce | flops 4096 | bytes 32768
  334.5 0.6 slice_bitcast_fusion.1
  335.1 0.6 pad_maximum_fusion.1
  335.6 0.6 slice_bitcast_fusion.2
  336.2 0.0 copy-done.1
  336.2 8.5 %convolution_add_fusion = f32[2048,512]{1,0:T(8,128)} fusion(f32[2048,512]{1,0:T(8,128)} %get-tuple-element.21, bf16[2048,1536]{1,0:T(8,128)(2,1)} %bitcast.39, bf16[512,1536]{1,0:T(8,128)(2,1)S(1)} %copy-done.1), kind=kOutput, calls=%fused_computation.4 | convolution fusion | flops 3222274048 | bytes 16252928 | tf_op jit(solution)/shard_map/dot_general | solution.py:23
  344.7 18.7 %reduce-scatter.9.cloned.1.call-done = f32[16,512]{1,0:T(8,128)} async-done(((f32[512,512]{1,0:T(8,128)}), f32[16,512]{1,0:T(8,128)}) %reduce-scatter.9.cloned.1.call-update) | async-done | bytes 32784 | tf_op jit(solution)/shard_map/reduce_scatter | solution.py:477
  363.4 104.3 %reduce-scatter.13.cloned.1.call-done = f32[16,1536]{1,0:T(8,128)} async-done(((f32[512,1536]{1,0:T(8,128)}), f32[16,1536]{1,0:T(8,128)}) %reduce-scatter.13.cloned.1.call-update) | async-done | bytes 98320
  467.6 142.7 %reduce-scatter.15.cloned.1.call-done = f32[16,2048]{1,0:T(8,128)} async-done(((f32[512,2048]{1,0:T(8,128)}), f32[16,2048]{1,0:T(8,128)}) %reduce-scatter.15.cloned.1.call-update) | async-done | bytes 131088
  610.3 139.8 %reduce-scatter.11.cloned.1.call-done = f32[64,512]{1,0:T(8,128)} async-done(((f32[2048,512]{1,0:T(8,128)}), f32[64,512]{1,0:T(8,128)}) %reduce-scatter.11.cloned.1.call-update) | async-done | bytes 131088 | tf_op jit(solution)/shard_map/reduce_scatter | solution.py:481
  (9 shorter events, 0.1 us)
Async XLA Ops:
  7.2 92.0 %all-gather.6.cloned.1.call-start = ((), (), s32[]{:S(2)}) async-start(), calls=%async_computation.4 | async-start | bytes 1622016 | tf_op jit(solution)/shard_map/all_gather | solution.py:424
  7.9 119.8 %all-gather.8.cloned.1.call-start = ((), (), s32[]{:S(2)}) async-start(), calls=%async_computation.5 | async-start | bytes 2162688 | tf_op jit(solution)/shard_map/all_gather | solution.py:426
  8.7 177.0 %all-gather.10.cloned.1.call-start = ((), (), s32[]{:S(2)}) async-start(), calls=%async_computation.6 | async-start | bytes 2162688 | tf_op jit(solution)/shard_map/all_gather | solution.py:427
  9.4 354.0 %reduce-scatter.9.cloned.1.call-start = ((), (), s32[]{:S(2)}) async-start(), calls=%async_computation.7 | async-start | bytes 1081344 | tf_op jit(solution)/shard_map/reduce_scatter | solution.py:477
  229.5 238.2 %reduce-scatter.13.cloned.1.call-start = ((), (), s32[]{:S(2)}) async-start(), calls=%async_computation.9 | async-start | bytes 3244032
  264.6 345.8 %reduce-scatter.15.cloned.1.call-start = ((), (), s32[]{:S(2)}) async-start(), calls=%async_computation.10 | async-start | bytes 4325376
  280.0 470.1 %reduce-scatter.11.cloned.1.call-start = ((), (), s32[]{:S(2)}) async-start(), calls=%async_computation.8 | async-start | bytes 4325376 | tf_op jit(solution)/shard_map/reduce_scatter | solution.py:481
  285.3 4.0 copy-start
  285.3 50.9 %copy-start.1 = (bf16[512,1536]{1,0:T(8,128)(2,1)S(1)}, bf16[512,1536]{1,0:T(8,128)(2,1)}, u32[]{:S(2)}) copy-start(bf16[512,1536]{1,0:T(8,128)(2,1)} %all-gather.6.cloned.1.call-done) | copy-start | bytes 4718596
Sparse Core Ops, SparseCore 0:
  10.9 58.1 all-gather.5
  71.9 55.5 all-gather.7
  130.4 55.2 all-gather.9
  229.6 133.7 reduce-scatter.8
  370.1 97.4 reduce-scatter.12
  470.4 139.8 reduce-scatter.14
  613.3 136.8 reduce-scatter.10

commit v2 on v1

--- a/solution.py
+++ b/solution.py
@@ -395,6 +395,608 @@
     )(tok, ctx, cot, mix, lift, drop, bias)
 
 
+MESH = pl.DeviceIdType.MESH
+
+
+class Place:
+    def __init__(self, nz):
+        self.nz = nz
+        self.z = lax.axis_index("gx")
+        g = lax.axis_index("gy")
+        self.c = g % 2
+        self.x = (g // 2) % 2
+        self.y = g // 4
+        self.oc = 1 - self.c
+        self.y1 = self.y + self.oc * (1 - 2 * self.y)
+        self.x1 = self.x + self.c * (1 - 2 * self.x)
+        self.y2 = self.y + self.c * (1 - 2 * self.y)
+        self.x2 = self.x + self.oc * (1 - 2 * self.x)
+        self.core = (self.z, self.y * 4 + self.x * 2 + self.oc)
+        self.near1 = (self.z, self.y1 * 4 + self.x1 * 2 + self.c)
+        self.near2 = (self.z, self.y2 * 4 + self.x2 * 2 + self.c)
+
+    def at_z(self, z):
+        return (z, self.y * 4 + self.x * 2 + self.c)
+
+    def up(self, k):
+        return (self.z + k) % self.nz
+
+    def down(self, k):
+        return (self.z + self.nz - k) % self.nz
+
+    def greet(self):
+        barrier = pltpu.get_barrier_semaphore()
+        others = [self.core, self.near1, self.near2] + [self.at_z(self.up(k)) for k in range(1, self.nz)]
+        for other in others:
+            pl.semaphore_signal(barrier, inc=1, device_id=other, device_id_type=MESH)
+        pl.semaphore_wait(barrier, len(others))
+
+
+def remote(src, dst, send, recv, u, k, device):
+    return pltpu.make_async_remote_copy(
+        src_ref=src,
+        dst_ref=dst,
+        send_sem=send.at[u, k],
+        recv_sem=recv.at[u, k],
+        device_id=device,
+        device_id_type=MESH,
+    )
+
+
+class Gather:
+    def __init__(self, me, buf, send, recv, u):
+        nz = me.nz
+        own = buf.at[:, me.y, me.x, me.c]
+        other = buf.at[:, me.y1, me.x1, me.c]
+        mine = buf.at[me.z, me.y, me.x, me.c]
+        half = buf.at[:, :, :, me.c]
+        self.along_z = lambda: [remote(mine, mine, send, recv, u, k - 1, me.at_z(me.up(k))) for k in range(1, nz)]
+        self.first = lambda: remote(own, own, send, recv, u, nz - 1, me.near1)
+        self.second = lambda: remote(own, own, send, recv, u, nz, me.near2)
+        self.passed = lambda: remote(other, other, send, recv, u, nz + 1, me.near2)
+        self.core = lambda: remote(half, half, send, recv, u, nz + 2, me.core)
+
+    def start(self):
+        for copy in self.along_z():
+            copy.start()
+
+    def step1(self):
+        for copy in self.along_z():
+            copy.wait_recv()
+        self.first().start()
+        self.second().start()
+
+    def step2(self):
+        self.first().wait_recv()
+        self.passed().start()
+
+    def step3(self):
+        self.second().wait_recv()
+        self.passed().wait_recv()
+        self.core().start()
+
+    def step4(self):
+        self.core().wait_recv()
+
+    def finish(self):
+        for copy in self.along_z() + [self.first(), self.second(), self.passed(), self.core()]:
+            copy.wait_send()
+
+
+class Reduce:
+    def __init__(self, me, bufs, u, send, recv):
+        self.me = me
+        nz = me.nz
+        self.sc, self.rc, self.s1, self.r1, self.s2, self.r2, self.sz, self.rz, self.hold = [b.at[u] for b in bufs]
+        self.core = lambda: remote(self.sc, self.rc, send, recv, u, 0, me.core)
+        self.first = lambda: remote(self.s1, self.r1, send, recv, u, 1, me.near2)
+        self.second = lambda: remote(self.s2, self.r2, send, recv, u, 2, me.near1)
+        self.along_z = lambda: [
+            remote(self.sz.at[me.up(k)], self.rz.at[me.z], send, recv, u, 2 + k, me.at_z(me.up(k)))
+            for k in range(1, nz)
+        ]
+
+    def start(self, unit):
+        me = self.me
+        self.sc[...] = unit[:, :, :, me.oc].astype(BF)
+        self.core().start()
+
+    def step1(self, unit):
+        me = self.me
+        self.core().wait_recv()
+
+        def total(y, x):
+            return unit[:, y, x, me.c] + self.rc[:, y, x].astype(F32)
+
+        self.s1[0] = total(me.y2, me.x2).astype(BF)
+        self.s1[1] = total(1 - me.y, 1 - me.x).astype(BF)
+        self.first().start()
+        self.hold[0] = total(me.y, me.x)
+        self.hold[1] = total(me.y1, me.x1)
+
+    def step2(self):
+        self.first().wait_recv()
+        self.s2[...] = (self.hold[1] + self.r1[1].astype(F32)).astype(BF)
+        self.second().start()
+        self.hold[0] = self.hold[0] + self.r1[0].astype(F32)
+
+    def step3(self):
+        self.second().wait_recv()
+        total = self.hold[0] + self.r2[...].astype(F32)
+        self.sz[...] = total.astype(BF)
+        self.hold[0] = total
+        for copy in self.along_z():
+            copy.start()
+
+    def step4(self):
+        me = self.me
+        for copy in self.along_z():
+            copy.wait_recv()
+        total = self.hold[0, me.z]
+        for k in range(1, me.nz):
+            total = total + self.rz[me.down(k)].astype(F32)
+        return total
+
+    def finish(self):
+        for copy in [self.core(), self.first(), self.second()] + self.along_z():
+            copy.wait_send()
+
+
+def reduce_bufs(n, nz, w):
+    return [
+        pltpu.VMEM((n, nz, 2, 2, 16, w), BF),
+        pltpu.VMEM((n, nz, 2, 2, 16, w), BF),
+        pltpu.VMEM((n, 2, nz, 16, w), BF),
+        pltpu.VMEM((n, 2, nz, 16, w), BF),
+        pltpu.VMEM((n, nz, 16, w), BF),
+        pltpu.VMEM((n, nz, 16, w), BF),
+        pltpu.VMEM((n, nz, 16, w), BF),
+        pltpu.VMEM((n, nz, 16, w), BF),
+        pltpu.VMEM((n, 2, nz, 16, w), F32),
+    ]
+
+
+def sems(n, nz):
+    return [pltpu.SemaphoreType.DMA((n, nz + 3)), pltpu.SemaphoreType.DMA((n, nz + 3))]
+
+
+def first_kernel(nz, tok_ref, own_ref, bias_own_ref, qkv_ref, w_ref, bias_ref, bw_ref, send, recv, bsend, brecv):
+    me = Place(nz)
+    units = own_ref.shape[0]
+    tokens, width = tok_ref.shape
+    for u in range(units):
+        w_ref[u, me.z, me.y, me.x, me.c] = own_ref[u]
+    bw_ref[0, me.z, me.y, me.x, me.c] = bias_own_ref[...]
+    me.greet()
+    jobs = [Gather(me, bw_ref.at[0], bsend, brecv, 0)] + [Gather(me, w_ref.at[u], send, recv, u) for u in range(units)]
+    for job in jobs:
+        job.start()
+    n = len(jobs)
+    for s in range(n + 3):
+        if s < n:
+            jobs[s].step1()
+        if 0 <= s - 1 < n:
+            jobs[s - 1].step2()
+        if 0 <= s - 2 < n:
+            jobs[s - 2].step3()
+        if 0 <= s - 3 < n:
+            jobs[s - 3].step4()
+            u = s - 4
+            if u < 0:
+                bias_ref[...] = bw_ref[0].reshape(512, 128).astype(F32).T[:8]
+            elif u < 3:
+
+                @pl.loop(0, tokens // 512)
+                def _(b, u=u):
+                    rows = pl.ds(pl.multiple_of(b * 512, 512), 512)
+                    y = mm(tok_ref[rows, :], w_ref[u].reshape(512, 512))
+                    if u == 0:
+                        y = y + bias_ref[6:7, :]
+                    if u == 2:
+                        y = y + bias_ref[7:8, :]
+                    qkv_ref[rows, u * 512 : (u + 1) * 512] = y.astype(BF)
+
+    for job in jobs:
+        job.finish()
+
+
+def first(nz, tok, own, bias_own):
+    units = own.shape[0]
+    tokens = tok.shape[0]
+    vmem = pl.BlockSpec(memory_space=pltpu.VMEM)
+    return pl.pallas_call(
+        functools.partial(first_kernel, nz),
+        in_specs=[vmem] * 3,
+        out_specs=[vmem] * 3,
+        out_shape=[
+            jax.ShapeDtypeStruct((tokens, 1536), BF),
+            jax.ShapeDtypeStruct((units, nz, 2, 2, 2, 16, 512), BF),
+            jax.ShapeDtypeStruct((8, 512), F32),
+        ],
+        scratch_shapes=[pltpu.VMEM((1, nz, 2, 2, 2, 16, 128), BF)] + sems(units, nz) + sems(1, nz),
+        compiler_params=pltpu.CompilerParams(vmem_limit_bytes=VMEM_LIMIT, collective_id=1, has_side_effects=True),
+        name="gather_joint",
+    )(tok, own, bias_own)
+
+
+def middle_kernel(
+    nz,
+    tb,
+    tok_ref,
+    ctx_ref,
+    cot_ref,
+    mix_ref,
+    early_ref,
+    own_ref,
+    bias_ref,
+    out_ref,
+    gmid_ref,
+    gctx_ref,
+    gmix_ref,
+    gbias_ref,
+    grad_ref,
+    w_ref,
+    hid_ref,
+    hidt_ref,
+    cott_ref,
+    acc_ref,
+    act_ref,
+    gl_ref,
+    gdt_ref,
+    sum_ref,
+    early_sem,
+    gsend,
+    grecv,
+    rsend,
+    rrecv,
+    *bufs,
+):
+    me = Place(nz)
+    tokens, width = tok_ref.shape
+    nf = w_ref.shape[0] // 2
+    nb = tokens // tb
+    early = early_ref.shape[0]
+    load = pltpu.make_async_copy(early_ref, w_ref.at[0:early], early_sem)
+    load.start()
+    ones = jnp.ones((16, tb), BF)
+
+    def gathers(f):
+        return [Gather(me, w_ref.at[2 * f + i], gsend, grecv, 2 * f + i) for i in range(2)]
+
+    def reduces(f):
+        return [Reduce(me, bufs, 2 * f + i, rsend, rrecv) for i in range(2)]
+
+    for u in range(early, 2 * nf):
+        w_ref[u, me.z, me.y, me.x, me.c] = own_ref[u - early]
+    me.greet()
+    for f in range(early // 2, nf):
+        for job in gathers(f):
+            job.start()
+
+    @pl.loop(0, nb)
+    def _(b):
+        rows = pl.ds(pl.multiple_of(b * tb, tb), tb)
+        mid = tok_ref[rows, :].astype(F32) + mm(ctx_ref[rows, :], mix_ref[...]) + bias_ref[5:6, :]
+        acc_ref[rows, :] = mid + bias_ref[4:5, :]
+        h = mid.astype(BF)
+        hid_ref[rows, :] = h
+        hidt_ref[0:width, rows] = h.T
+        hidt_ref[width : width + 16, rows] = ones
+        c = cot_ref[rows, :]
+        cott_ref[:, rows] = c.T
+        gmid_ref[rows, :] = c.astype(F32)
+
+    gbias_ref[...] = jnp.zeros_like(gbias_ref)
+    load.wait()
+
+    def lift(f):
+        return w_ref.at[2 * f]
+
+    def drop(f):
+        return w_ref.at[2 * f + 1]
+
+    def stage1(f, b):
+        rows = pl.ds(b * tb, tb)
+        lw = w_ref[2 * f].reshape(512, 512)
+        dw = w_ref[2 * f + 1].reshape(512, 512)
+        for n in range(0, 512, 256):
+            x = mm(hid_ref[rows, :], lw[:, n : n + 256]) + bias_ref[pl.ds(f, 1), n : n + 256]
+            grad = mm(cot_ref[rows, :], dw[n : n + 256, :], NT)
+            a, g = gelu_pair(x, grad)
+            act_ref[b, :, n : n + 256] = a
+            gl_ref[b, :, n : n + 256] = g
+
+    def stage2(f, b):
+        slot = f % 2
+        rows = pl.ds(b * tb, tb)
+        act = act_ref[b]
+        gl = gl_ref[b]
+        acc_ref[rows, :] += mm(act, w_ref[2 * f + 1].reshape(512, 512))
+        gmid_ref[rows, :] += mm(gl, w_ref[2 * f].reshape(512, 512), NT)
+        gd = mm(cott_ref[:, rows], act)
+        gf = mm(hidt_ref[:, rows], gl)
+        unit = gf[:width].reshape(nz, 2, 2, 2, 16, 512)
+        if b == 0:
+            gdt_ref[...] = gd
+            sum_ref[slot, 0] = unit
+        elif b < nb - 1:
+            gdt_ref[...] += gd
+            sum_ref[slot, 0] += unit
+        else:
+            sum_ref[slot, 1] = (gdt_ref[...] + gd).T.reshape(nz, 2, 2, 2, 16, 512)
+            sum_ref[slot, 0] += unit
+        gbias_ref[pl.ds(f, 1), :] += gf[width : width + 1]
+
+    def reduce_step(f, k):
+        slot = f % 2
+        for i, job in enumerate(reduces(f)):
+            if k == 0:
+                job.start(sum_ref.at[slot, i])
+            elif k == 1:
+                job.step1(sum_ref.at[slot, i])
+            elif k == 2:
+                job.step2()
+            elif k == 3:
+                job.step3()
+            else:
+                grad_ref[2 * f + i] = job.step4()
+
+    def gather_step(f, k):
+        for job in gathers(f):
+            (job.step1, job.step2, job.step3, job.step4)[k]()
+
+    @pl.loop(0, nf)
+    def _(f):
+        for k in range(nb):
+
+            @pl.when(f > 0)
+            def _(k=k):
+                if k == 0:
+                    gather_step(f, 3)
+                reduce_step(f - 1, k)
+
+            @pl.when(f + 1 < nf)
+            def _(k=k):
+                if k < 3:
+                    gather_step(f + 1, k)
+
+            if k == 0:
+
+                @pl.when(f > 1)
+                def _():
+                    reduce_step(f - 2, 4)
+
+            stage1(f, k)
+            if k > 0:
+                stage2(f, k - 1)
+        stage2(f, nb - 1)
+
+    gmix_ref[...] = jnp.zeros_like(gmix_ref)
+    for b in range(nb):
+        if b == 0:
+            reduce_step(nf - 2, 4)
+        reduce_step(nf - 1, b)
+        rows = pl.ds(b * tb, tb)
+        out_ref[rows, :] = acc_ref[rows, :].astype(BF)
+        gb = gmid_ref[rows, :].astype(BF)
+        gctx_ref[rows, :] = mm(gb, mix_ref[...], NT).astype(BF)
+        gmix_ref[...] += mm(ctx_ref[rows, :].T, gb)
+        gbias_ref[5:6, :] += mm(ones, gb)[0:1]
+        gbias_ref[4:5, :] += mm(ones, cot_ref[rows, :])[0:1]
+    reduce_step(nf - 1, 4)
+    for f in range(nf):
+        if f >= early // 2:
+            for job in gathers(f):
+                job.finish()
+        for job in reduces(f):
+            job.finish()
+
+
+def middle(nz, tok, ctx, cot, mix, early, own, bias):
+    tokens, width = tok.shape
+    n = early.shape[0] + own.shape[0]
+    tb = tokens // 4
+    vmem = pl.BlockSpec(memory_space=pltpu.VMEM)
+    return pl.pallas_call(
+        functools.partial(middle_kernel, nz, tb),
+        in_specs=[vmem] * 4 + [pl.BlockSpec(memory_space=pl.ANY)] + [vmem] * 2,
+        out_specs=[vmem] * 6,
+        out_shape=[
+            jax.ShapeDtypeStruct((tokens, width), BF),
+            jax.ShapeDtypeStruct((tokens, width), F32),
+            jax.ShapeDtypeStruct((tokens, width), BF),
+            jax.ShapeDtypeStruct((width, width), F32),
+            jax.ShapeDtypeStruct((8, 512), F32),
+            jax.ShapeDtypeStruct((n, 16, 512), F32),
+        ],
+        scratch_shapes=[
+            pltpu.VMEM((n, nz, 2, 2, 2, 16, 512), BF),
+            pltpu.VMEM((tokens, width), BF),
+            pltpu.VMEM((width + 16, tokens), BF),
+            pltpu.VMEM((width, tokens), BF),
+            pltpu.VMEM((tokens, width), F32),
+            pltpu.VMEM((4, tb, 512), BF),
+            pltpu.VMEM((4, tb, 512), BF),
+            pltpu.VMEM((width, 512), F32),
+            pltpu.VMEM((2, 2, nz, 2, 2, 2, 16, 512), F32),
+            pltpu.SemaphoreType.DMA,
+        ]
+        + sems(n, nz)
+        + sems(n, nz)
+        + reduce_bufs(n, nz, 512),
+        compiler_params=pltpu.CompilerParams(vmem_limit_bytes=VMEM_LIMIT, collective_id=2, has_side_effects=True),
+        name="feed",
+    )(tok, ctx, cot, mix, early, own, bias)
+
+
+def last_kernel(
+    nz,
+    tok_ref,
+    gj_ref,
+    gmid_ref,
+    jw_ref,
+    gmix_ref,
+    gbias_ref,
+    tg_ref,
+    own_ref,
+    obias_ref,
+    tokt_ref,
+    sum_ref,
+    bsum_ref,
+    brow_ref,
+    send,
+    recv,
+    bsend,
+    brecv,
+    *bufs,
+):
+    me = Place(nz)
+    tokens, width = tok_ref.shape
+    me.greet()
+    jobs = [Reduce(me, bufs[:9], u, send, recv) for u in range(4)] + [Reduce(me, bufs[9:], 0, bsend, brecv)]
+    units = [gmix_ref] + [sum_ref.at[j] for j in range(3)] + [bsum_ref]
+    n = 5
+    jobs[0].start(units[0])
+
+    @pl.loop(0, tokens // 512)
+    def _(b):
+        rows = pl.ds(pl.multiple_of(b * 512, 512), 512)
+        tokt_ref[0:width, rows] = tok_ref[rows, :].T
+        tokt_ref[width : width + 16, rows] = jnp.ones((16, 512), BF)
+
+    def token_block(b):
+        rows = pl.ds(pl.multiple_of(b * 512, 512), 512)
+        total = gmid_ref[rows, :]
+        for j in range(3):
+            total = total + mm(gj_ref[rows, j * 512 : (j + 1) * 512], jw_ref[j], NT)
+        tg_ref[rows, :] = total
+
+    brow_ref[...] = jnp.zeros_like(brow_ref)
+    brow_ref[0:8, :] = gbias_ref[...]
+    done = 0
+    for s in range(n + 4):
+        if 0 <= s - 4 < n:
+            u = s - 4
+            total = jobs[u].step4()
+            if u < 4:
+                own_ref[u] = total
+            else:
+                obias_ref[...] = total
+        if 0 <= s - 3 < n:
+            jobs[s - 3].step3()
+        if 0 <= s - 2 < n:
+            jobs[s - 2].step2()
+        if 0 <= s - 1 < n:
+            jobs[s - 1].step1(units[s - 1])
+        if s < 3:
+            g = mm(tokt_ref[...], gj_ref[:, s * 512 : (s + 1) * 512])
+            sum_ref[s] = g[:width].reshape(nz, 2, 2, 2, 16, 512)
+            if s != 1:
+                brow_ref[6 + s // 2 : 7 + s // 2, :] = g[width : width + 1]
+            jobs[s + 1].start(units[s + 1])
+        elif s == 3:
+            bsum_ref[...] = brow_ref[...].T.reshape(nz, 2, 2, 2, 16, 128)
+            jobs[4].start(units[4])
+        if s >= 3 and done < tokens // 512:
+            token_block(done)
+            done += 1
+    while done < tokens // 512:
+        token_block(done)
+        done += 1
+    for job in jobs:
+        job.finish()
+
+
+def last(nz, tok, gj, gmid, jw, gmix, gbias):
+    tokens, width = tok.shape
+    vmem = pl.BlockSpec(memory_space=pltpu.VMEM)
+    return pl.pallas_call(
+        functools.partial(last_kernel, nz),
+        in_specs=[vmem] * 6,
+        out_specs=[vmem] * 3,
+        out_shape=[
+            jax.ShapeDtypeStruct((tokens, width), F32),
+            jax.ShapeDtypeStruct((4, 16, 512), F32),
+            jax.ShapeDtypeStruct((16, 128), F32),
+        ],
+        scratch_shapes=[
+            pltpu.VMEM((width + 16, tokens), BF),
+            pltpu.VMEM((3, nz, 2, 2, 2, 16, 512), F32),
+            pltpu.VMEM((nz, 2, 2, 2, 16, 128), F32),
+            pltpu.VMEM((128, 512), F32),
+        ]
+        + sems(4, nz)
+        + sems(1, nz)
+        + reduce_bufs(4, nz, 512)
+        + reduce_bufs(1, nz, 128),
+        compiler_params=pltpu.CompilerParams(vmem_limit_bytes=VMEM_LIMIT, collective_id=3, has_side_effects=True),
+        name="joint_grads",
+    )(tok, gj, gmid, jw, gmix.reshape(nz, 2, 2, 2, 16, 512), gbias)
+
+
+EARLY = 2
+
+
+def remote_body(
+    tokens,
+    segment_ids,
+    fill_lengths,
+    joint_weight,
+    joint_bias,
+    mix_weight,
+    mix_bias,
+    lift_weight,
+    lift_bias,
+    drop_weight,
+    drop_bias,
+    cotangent,
+):
+    rows, length, width = tokens.shape
+    nz = lax.axis_size("gx")
+    n_tok = rows * length
+    tok = tokens.reshape(n_tok, width)
+    cot = cotangent.reshape(n_tok, width)
+    seg = segment_ids.reshape(rows, 1, length)
+    starts = jnp.sum(
+        segment_ids[:, None, :] < jnp.arange(8, dtype=jnp.int32)[None, :, None], axis=-1, dtype=jnp.int32
+    )
+    nf = drop_weight.shape[0] // 16
+    lift_own = lift_weight.reshape(16, -1, nf, 16).transpose(2, 0, 1, 3).reshape(nf, 16, 512)
+    drop_own = drop_weight.reshape(nf, 16, 512)
+    joint_own = joint_weight.reshape(16, 3, 512).transpose(1, 0, 2)
+    feed_own = jnp.stack([lift_own, drop_own], axis=1).reshape(2 * nf, 16, 512)
+    first_own = jnp.concatenate([joint_own, mix_weight[None], feed_own[:EARLY]])
+    bias_own = jnp.concatenate([lift_bias.reshape(nf, 16), drop_bias[None], mix_bias[None], joint_bias])
+    bias_own = jnp.pad(bias_own, ((0, 120), (0, 0))).T
+
+    qkv, weights, bias = first(nz, tok, first_own, bias_own)
+    qkv3 = qkv.reshape(rows, length, 3 * width)
+    ctx, lse = attend(starts, fill_lengths, seg, qkv3)
+    out, gmid, gctx, gmix, gbias, feed_grads = middle(
+        nz, tok, ctx.reshape(n_tok, width), cot, weights[3].reshape(width, width), weights[4:], feed_own[EARLY:], bias
+    )
+    gjoint = attend_back(
+        starts, fill_lengths, seg, qkv3, lse, ctx, gctx.reshape(rows, length, width)
+    ).reshape(n_tok, 3 * width)
+    token_grad, grads, gb = last(nz, tok, gjoint, gmid, weights[:3].reshape(3, width, width), gmix, gbias)
+    feed_grads = feed_grads.reshape(nf, 2, 16, 512)
+    glift = feed_grads[:, 0].reshape(nf, 16, -1, 16).transpose(1, 2, 0, 3).reshape(16, nf * 512)
+    gdrop = feed_grads[:, 1].reshape(nf * 16, 512)
+    gb = gb[:, :8].T
+    return (
+        out.reshape(rows, length, width),
+        token_grad.reshape(rows, length, width),
+        grads[1:4].transpose(1, 0, 2).reshape(16, 3 * width),
+        gb[6:8],
+        grads[0],
+        gb[5],
+        glift,
+        gb[:nf].reshape(-1),
+        gdrop,
+        gb[4],
+    )
+
+
 BOTH = ("gx", "gy")
 
 
@@ -490,4 +1092,5 @@
     bias = P(None, BOTH)
     in_specs = (wide, rows, flat, rows, bias, rows, flat, rows, flat, rows, flat, wide)
     out_specs = (wide, wide, rows, bias, rows, flat, rows, flat, rows, flat)
-    return jax.shard_map(body, mesh=mesh, in_specs=in_specs, out_specs=out_specs, check_vma=False)
+    fits = mesh.shape["gy"] == 8 and mesh.shape["gx"] == 4
+    return jax.shard_map(remote_body if fits else body, mesh=mesh, in_specs=in_specs, out_specs=out_specs, check_vma=False)

time: 762 us -> 265 us (0.35)
  waiting for transfers between devices: 460 us -> 0 us
  Pallas kernels: 90.6 us -> 232 us
  blocking collectives: 129 us -> 0 us
  matrix products: 22.8 us -> 0 us
  between operations: 14.5 us -> 1 us
    unnamed x9 -> x0, waiting for transfers between devices: 249 us -> none
    reduce_scatter x2 -> x0, waiting for transfers between devices: 158 us -> none  [the longest x1 140 us: body(): scatter(gdrop_w)]
    pallas_call x1 -> x3, Pallas kernels: 43.8 us -> 175 us  [the longest x1 92.4 us: middle(): pl.pallas_call(functools.partial(middle_kernel, nz, tb), in_specs=[vmem]...]
    all_gather x2 -> x0, blocking collectives: 84 us -> none  [the longest x1 43 us: body(): all_bias = lax.all_gather(own_bias, BOTH, axis=0)]
    all_gather x3 -> x0, waiting for transfers between devices: 52.7 us -> none  [the longest x1 52.7 us: body(): drop_w = lax.all_gather(drop_weight, BOTH, axis=0, tiled=True)]
    unnamed x1 -> x0, blocking collectives: 44.8 us -> none
    dot_general x3 -> x0, matrix products: 22.8 us -> none  [the longest x2 16.6 us: mm(): return lax.dot_general(a, b, dims, preferred_element_type=F32)]
    transpose x3, local copies, waits for them, and re-layouts: 15.1 us -> 1.49 us  [the longest x1 0.71 us: remote_body(): feed_grads[:, 0].reshape(nf, 16, -1, 16).transpose(1, 2, 0, 3)]
  transfers between devices with their start and end apart: 7 -> 0, of which waited for: 5 -> 0; matrix products, arithmetic and copies ran while one was open for 8% -> 0% of each run, Pallas kernels for 6% -> 0%
where the time goes in v2:
time: 265 us; the launch traced here: 264 us
  Pallas kernels  232 us (88%)
  local copies, waits for them, and re-layouts  27.1 us (10%)
  other arithmetic  3.43 us (1%)
    pallas_call x1, Pallas kernels, middle(): pl.pallas_call(functools.partial(middle_kernel, nz, tb), in_specs=[vmem]...  92.4 us
    pallas_call x1, Pallas kernels, last(): pl.pallas_call(functools.partial(last_kernel, nz), in_specs=[vmem] * 6, o...  44.8 us
    pallas_call x1, Pallas kernels, first(): pl.pallas_call(functools.partial(first_kernel, nz), in_specs=[vmem] * 3,...  38 us
    pallas_call x1, Pallas kernels, attend_back(): pl.pallas_call(functools.partial(attend_back_kernel, length=length), grid...  36.5 us
    pallas_call x1, Pallas kernels, attend(): pl.pallas_call(functools.partial(attend_kernel, length=length), grid_spec...  20.3 us
    unnamed x15, local copies, waits for them, and re-layouts  7.52 us

profile of v2, /device:TPU:0, one launch (start us, length us, event | category | flops | bytes accessed | tf_op | source)
XLA Modules:
  0.0 263.6 jit_solution(3384826435277877401)
XLA Ops:
  0.6 0.0 copy-start.2
  0.7 0.0 copy-start.4
  0.7 1.4 convert_reduce_fusion.starts_ref
  2.1 0.7 reshape.79
  2.8 0.1 copy.45
  2.9 0.7 copy.48
  3.7 0.7 copy.47
  4.4 0.7 copy.46
  5.2 0.7 fusion.7.bias_own_ref
  5.9 1.3 broadcast_in_dim.13.seg_ref
  7.2 0.8 copy.58
  8.0 1.2 reshape.78
  9.2 0.1 copy.43
  9.3 0.8 stack_reshape.6
  10.1 0.0 copy-done.2
  10.1 0.0 copy-done.4
  10.1 0.7 pad_maximum_fusion.1.own_ref
  10.7 0.7 pad_maximum_fusion
  11.4 38.0 %gather_joint.1 = (bf16[2048,1536]{1,0:T(8,128)(2,1)}, bf16[6,4,2,2,2,16,512]{6,5,4,3,2,1,0:T(8,128)(2,1)}, f32[8,512]{1,0:T(8,128)}) custom-call(bf16[2048,512]{1,0:T(8,128)(2,1)} %bitcast.52, bf16[6,16,512]{2,1,0:T(8,128)(2,1)} %pad_maximum_fusion.1.own_ref, bf16[16,128]{1,0:T(8,128)(2,1)} %fusion.7.bias_own_ref), custom_call_target="tpu_custom_call" | custom-call | tf_op jit(solution)/shard_map/gather_joint/pallas_call | solution.py:607
  49.5 0.0 copy-start.1
  49.5 2.1 slice.50
  51.5 2.3 slice.51.early_ref
  53.8 0.0 copy-done.1
  53.8 1.3 slice.54
  55.1 20.3 %attend.1 = (bf16[2,1024,512]{2,1,0:T(8,128)(2,1)}, f32[2,4,8,256]{3,2,1,0:T(8,128)}) custom-call(s32[2,8]{1,0:T(2,128)} %convert_reduce_fusion.starts_ref, s32[2]{0:T(128)} %fill_ref.3, s32[2,1,1024]{2,1,0:T(1,128)} %broadcast_in_dim.13.seg_ref, bf16[2,1024,1536]{2,1,0:T(8,128)(2,1)} %bitcast.49), custom_call_target="tpu_custom_call" | custom-call | tf_op jit(solution)/shard_map/attend/pallas_call | solution.py:128
  75.3 92.4 %feed.1 = (bf16[2048,512]{1,0:T(8,128)(2,1)}, f32[2048,512]{1,0:T(8,128)}, bf16[2048,512]{1,0:T(8,128)(2,1)}, f32[512,512]{1,0:T(8,128)}, f32[8,512]{1,0:T(8,128)}, /*index=5*/f32[8,16,512]{2,1,0:T(8,128)}) custom-call(bf16[2048,512]{1,0:T(8,128)(2,1)} %bitcast.53, bf16[2048,512]{1,0:T(8,128)(2,1)} %bitcast.55, bf16[2048,512]{1,0:T(8,128)(2,1)} %bitcast.62, ...), custom_call_target="tpu_custom_call" | custom-call | tf_op jit(solution)/shard_map/feed/pallas_call | solution.py:800
  167.7 36.5 %attend_back.1 = bf16[2,1024,1536]{2,1,0:T(8,128)(2,1)} custom-call(s32[2,8]{1,0:T(2,128)} %convert_reduce_fusion.starts_ref, s32[2]{0:T(128)} %fill_ref.3, s32[2,1,1024]{2,1,0:T(1,128)} %broadcast_in_dim.13.seg_ref, bf16[2,1024,1536]{2,1,0:T(8,128)(2,1)} %bitcast.50, f32[2,4,8,256]{3,2,1,0:T(8,128)} %get-tuple-element.29.lse_ref, ...), custom_call_target="tpu_custom_call" | custom-call | tf_op jit(solution)/shard_map/attend_back/pallas_call | solution.py:239
  204.2 0.0 copy-start.3
  204.3 44.8 %joint_grads.1 = (f32[2048,512]{1,0:T(8,128)}, f32[4,16,512]{2,1,0:T(8,128)}, f32[16,128]{1,0:T(8,128)}) custom-call(bf16[2048,512]{1,0:T(8,128)(2,1)} %bitcast.54, bf16[2048,1536]{1,0:T(8,128)(2,1)} %bitcast.51, f32[2048,512]{1,0:T(8,128)} %get-tuple-element.31.gmid_ref, bf16[3,512,512]{2,1,0:T(8,128)(2,1)} %bitcast.56, f32[4,2,2,2,16,512]{5,4,3,2,1,0:T(8,128)} %bitcast.64, ...), custom_call_target="tpu_custom_call" | custom-call | tf_op jit(solution)/shard_map/joint_grads/pallas_call | solution.py:913
  249.0 0.7 slice_bitcast_fusion.3
  249.7 0.7 slice_reduce_fusion
  250.4 0.1 copy.52
  250.5 0.6 reshape.92
  251.1 0.1 slice.64
  251.2 0.6 copy.53
  251.8 1.4 slice_bitcast_fusion.2
  253.2 0.9 slice_bitcast_fusion.1
  254.1 0.6 copy.56
  254.8 0.0 copy-done.3
  254.8 0.7 fusion.8
  255.4 0.4 reshape_squeeze.10
  255.8 0.7 copy.51
  256.5 1.6 reshape.91
  258.1 0.0 copy-start
  258.1 3.2 %copy.61 = bf16[2,1024,512]{2,1,0:T(8,128)(2,1)} copy(bf16[2,1024,512]{2,1,0:T(8,128)(2,1)} %bitcast.60) | data formatting | bytes 4194304
  261.3 0.0 copy-done
  261.3 2.0 copy.62
  (1 shorter events, 0.0 us)
Async XLA Ops:
  0.6 9.4 %copy-start.2 = (bf16[64,512]{1,0:T(8,128)(2,1)S(1)}, bf16[64,512]{1,0:T(8,128)(2,1)}, u32[]{:S(2)}) copy-start(bf16[64,512]{1,0:T(8,128)(2,1)} %param.21) | copy-start | bytes 196612
  0.7 9.4 %copy-start.4 = (bf16[16,512]{1,0:T(8,128)(2,1)S(1)}, bf16[16,512]{1,0:T(8,128)(2,1)}, u32[]{:S(2)}) copy-start(bf16[16,512]{1,0:T(8,128)(2,1)} %param.17) | copy-start | bytes 49156
  49.5 4.4 %copy-start.1 = (bf16[6,4,2,2,2,16,512]{6,5,4,3,2,1,0:T(8,128)(2,1)S(1)}, bf16[6,4,2,2,2,16,512]{6,5,4,3,2,1,0:T(8,128)(2,1)}, u32[]{:S(2)}) copy-start(bf16[6,4,2,2,2,16,512]{6,5,4,3,2,1,0:T(8,128)(2,1)} %get-tuple-element.26) | copy-start | bytes 9437188
  204.2 50.5 %copy-start.3 = (f32[8,16,512]{2,1,0:T(8,128)S(1)}, f32[8,16,512]{2,1,0:T(8,128)}, u32[]{:S(2)}) copy-start(f32[8,16,512]{2,1,0:T(8,128)} %get-tuple-element.37) | copy-start | bytes 786436
  258.1 3.2 %copy-start = (f32[2048,512]{1,0:T(8,128)S(1)}, f32[2048,512]{1,0:T(8,128)}, u32[]{:S(2)}) copy-start(f32[2048,512]{1,0:T(8,128)} %get-tuple-element.34) | copy-start | bytes 12582916

commit v3 on v2

--- a/solution.py
+++ b/solution.py
@@ -51,8 +51,14 @@
     return lo_b, (hi + 127) // 128 - lo_b
 
 
-def write_mask(mask_ref, segk_ref, seg_ref, fill, t, lo_b, n):
-    segq = seg_ref[0, :, pl.ds(pl.multiple_of(t * 128, 128), 128)]
+def ids_of(seg_ref, row, lanes):
+    ids = seg_ref[:, lanes]
+    mine = lax.broadcasted_iota(jnp.int32, ids.shape, 0) == row
+    return jnp.sum(jnp.where(mine, ids.astype(F32), 0.0), axis=0, keepdims=True)
+
+
+def write_mask(mask_ref, segk_ref, seg_ref, row, fill, t, lo_b, n):
+    segq = ids_of(seg_ref, row, pl.ds(pl.multiple_of(t * 128, 128), 128))
     segq = jnp.broadcast_to(segq, (128, 128))
     qi = t * 128 + lax.broadcasted_iota(jnp.int32, (128, 128), 1)
     ki0 = lax.broadcasted_iota(jnp.int32, (128, 128), 0)
@@ -63,10 +69,10 @@
         mask_ref[c * 128 : (c + 1) * 128, :] = jnp.where(ok, 0.0, NEG)
 
 
-def spread_segments(seg_ref, segk_ref, length):
+def spread_segments(seg_ref, segk_ref, row, length):
     for b in range(length // 128):
-        row = seg_ref[0, :, b * 128 : (b + 1) * 128].astype(F32)
-        segk_ref[b * 128 : (b + 1) * 128, :] = jnp.broadcast_to(row, (128, 128)).T.astype(jnp.int32)
+        ids = ids_of(seg_ref, row, slice(b * 128, (b + 1) * 128))
+        segk_ref[b * 128 : (b + 1) * 128, :] = jnp.broadcast_to(ids, (128, 128)).T
 
 
 def attend_kernel(
@@ -74,7 +80,7 @@
 ):
     row = pl.program_id(0)
     fill = fill_ref[row]
-    spread_segments(seg_ref, segk_ref, length)
+    spread_segments(seg_ref, segk_ref, row, length)
     for b in range(length // 128):
         for p in range(4):
             v = qkv_ref[0, b * 128 : (b + 1) * 128, 1024 + p * 128 : 1024 + (p + 1) * 128]
@@ -118,7 +124,7 @@
 
             @pl.when(n == k)
             def _(k=k):
-                write_mask(mask_ref, segk_ref, seg_ref, fill, t, lo_b, k)
+                write_mask(mask_ref, segk_ref, seg_ref, row, fill, t, lo_b, k)
                 tile(t, lo_b, k)
 
 
@@ -131,7 +137,7 @@
             num_scalar_prefetch=2,
             grid=(rows,),
             in_specs=[
-                pl.BlockSpec((1, 1, length), lambda r, *_: (r, 0, 0)),
+                pl.BlockSpec((rows, length), lambda r, *_: (0, 0)),
                 pl.BlockSpec((1, length, 1536), lambda r, *_: (r, 0, 0)),
             ],
             out_specs=[
@@ -140,7 +146,7 @@
             ],
             scratch_shapes=[
                 pltpu.VMEM((512, length), BF),
-                pltpu.VMEM((length, 128), jnp.int32),
+                pltpu.VMEM((length, 128), F32),
                 pltpu.VMEM((length, 128), F32),
                 pltpu.VMEM((4, length, 256), F32),
                 pltpu.VMEM((4, length, 256), BF),
@@ -163,7 +169,12 @@
     lse_ref,
     ctx_ref,
     do_ref,
+    gmid_ref,
+    jw_ref,
+    pass_ref,
     out_ref,
+    tg_ref,
+    to_ref,
     kt_ref,
     segk_ref,
     mask_ref,
@@ -176,7 +187,8 @@
 ):
     row = pl.program_id(0)
     fill = fill_ref[row]
-    spread_segments(seg_ref, segk_ref, length)
+    to_ref[...] = pass_ref[...]
+    spread_segments(seg_ref, segk_ref, row, length)
     for b in range(length // 128):
         for p in range(4):
             k = qkv_ref[0, b * 128 : (b + 1) * 128, 512 + p * 128 : 512 + (p + 1) * 128]
@@ -226,32 +238,43 @@
 
             @pl.when(n == k)
             def _(k=k):
-                write_mask(mask_ref, segk_ref, seg_ref, fill, t, lo_b, k)
+                write_mask(mask_ref, segk_ref, seg_ref, row, fill, t, lo_b, k)
                 tile(t, lo_b, k)
 
-    out_ref[0, :, 512:1024] = dk_ref[...].astype(BF)
-    out_ref[0, :, 1024:1536] = dv_ref[...].astype(BF)
-
-
-def attend_back(starts, fill, seg, qkv, lse, ctx, do):
+    for b in range(0, length, 256):
+        rows = slice(b, b + 256)
+        dk = dk_ref[rows, :].astype(BF)
+        dv = dv_ref[rows, :].astype(BF)
+        out_ref[0, rows, 512:1024] = dk
+        out_ref[0, rows, 1024:1536] = dv
+        total = gmid_ref[0, rows, :] + mm(out_ref[0, rows, 0:512], jw_ref[0], NT)
+        tg_ref[0, rows, :] = total + mm(dk, jw_ref[1], NT) + mm(dv, jw_ref[2], NT)
+
+
+def attend_back(starts, fill, seg, qkv, lse, ctx, do, gmid, joint, passed):
     rows, length, _ = qkv.shape
     blocks = length // 128
+    wide = pl.BlockSpec((1, length, 512), lambda r, *_: (r, 0, 0))
+    joined = pl.BlockSpec((1, length, 1536), lambda r, *_: (r, 0, 0))
     return pl.pallas_call(
         functools.partial(attend_back_kernel, length=length),
         grid_spec=pltpu.PrefetchScalarGridSpec(
             num_scalar_prefetch=2,
             grid=(rows,),
             in_specs=[
-                pl.BlockSpec((1, 1, length), lambda r, *_: (r, 0, 0)),
-                pl.BlockSpec((1, length, 1536), lambda r, *_: (r, 0, 0)),
+                pl.BlockSpec((rows, length), lambda r, *_: (0, 0)),
+                joined,
                 pl.BlockSpec((1, 4, blocks, 256), lambda r, *_: (r, 0, 0, 0)),
-                pl.BlockSpec((1, length, 512), lambda r, *_: (r, 0, 0)),
-                pl.BlockSpec((1, length, 512), lambda r, *_: (r, 0, 0)),
+                wide,
+                wide,
+                wide,
+                pl.BlockSpec((3, 512, 512), lambda r, *_: (0, 0, 0)),
+                wide,
             ],
-            out_specs=pl.BlockSpec((1, length, 1536), lambda r, *_: (r, 0, 0)),
+            out_specs=[joined, wide, wide],
             scratch_shapes=[
                 pltpu.VMEM((512, length), BF),
-                pltpu.VMEM((length, 128), jnp.int32),
+                pltpu.VMEM((length, 128), F32),
                 pltpu.VMEM((length, 128), F32),
                 pltpu.VMEM((length, 512), F32),
                 pltpu.VMEM((length, 512), F32),
@@ -259,10 +282,14 @@
                 pltpu.VMEM((4, length, 256), BF),
             ],
         ),
-        out_shape=jax.ShapeDtypeStruct((rows, length, 1536), BF),
+        out_shape=[
+            jax.ShapeDtypeStruct((rows, length, 1536), BF),
+            jax.ShapeDtypeStruct((rows, length, 512), F32),
+            jax.ShapeDtypeStruct(passed.shape, passed.dtype),
+        ],
         compiler_params=pltpu.CompilerParams(vmem_limit_bytes=VMEM_LIMIT),
         name="attend_back",
-    )(starts, fill, seg, qkv, lse, ctx, do)
+    )(starts, fill, seg, qkv, lse, ctx, do, gmid, joint, passed)
 
 
 def gelu_pair(x, grad):
@@ -396,6 +423,9 @@
 
 
 MESH = pl.DeviceIdType.MESH
+GATHER_TICKS = (0, 6, 10, 14, 16)
+REDUCE_TICKS = (0, 3, 8, 13, 17)
+EARLY = 4
 
 
 class Place:
@@ -560,63 +590,111 @@
     return [pltpu.SemaphoreType.DMA((n, nz + 3)), pltpu.SemaphoreType.DMA((n, nz + 3))]
 
 
-def first_kernel(nz, tok_ref, own_ref, bias_own_ref, qkv_ref, w_ref, bias_ref, bw_ref, send, recv, bsend, brecv):
+def unit_order():
+    c = lax.broadcasted_iota(jnp.int32, (512, 512), 1)
+    s = lax.broadcasted_iota(jnp.int32, (512, 512), 0)
+    return jnp.where(s == ((c & 127) >> 4) * 64 + (c >> 7) * 16 + (c & 15), 1.0, 0.0).astype(BF)
+
+
+def first_kernel(
+    nz,
+    tok_ref,
+    joint_ref,
+    mix_own_ref,
+    lift_ref,
+    drop_ref,
+    bias_own_ref,
+    seg_ref,
+    qkv_ref,
+    jw_ref,
+    mix_ref,
+    early_ref,
+    bias_ref,
+    starts_ref,
+    bw_ref,
+    send,
+    recv,
+):
     me = Place(nz)
-    units = own_ref.shape[0]
     tokens, width = tok_ref.shape
-    for u in range(units):
-        w_ref[u, me.z, me.y, me.x, me.c] = own_ref[u]
-    bw_ref[0, me.z, me.y, me.x, me.c] = bias_own_ref[...]
+    early = early_ref.shape[0]
+    nf = drop_ref.shape[0] // 16
+    here = (me.z, me.y, me.x, me.c)
+    bw_ref[here] = bias_own_ref[...]
+    for u in range(3):
+        jw_ref[(u,) + here] = joint_ref[:, u * 512 : (u + 1) * 512]
+    mix_ref[here] = mix_own_ref[...]
     me.greet()
-    jobs = [Gather(me, bw_ref.at[0], bsend, brecv, 0)] + [Gather(me, w_ref.at[u], send, recv, u) for u in range(units)]
-    for job in jobs:
-        job.start()
-    n = len(jobs)
-    for s in range(n + 3):
-        if s < n:
-            jobs[s].step1()
-        if 0 <= s - 1 < n:
-            jobs[s - 1].step2()
-        if 0 <= s - 2 < n:
-            jobs[s - 2].step3()
-        if 0 <= s - 3 < n:
-            jobs[s - 3].step4()
-            u = s - 4
-            if u < 0:
-                bias_ref[...] = bw_ref[0].reshape(512, 128).astype(F32).T[:8]
-            elif u < 3:
-
-                @pl.loop(0, tokens // 512)
-                def _(b, u=u):
-                    rows = pl.ds(pl.multiple_of(b * 512, 512), 512)
-                    y = mm(tok_ref[rows, :], w_ref[u].reshape(512, 512))
-                    if u == 0:
-                        y = y + bias_ref[6:7, :]
-                    if u == 2:
-                        y = y + bias_ref[7:8, :]
-                    qkv_ref[rows, u * 512 : (u + 1) * 512] = y.astype(BF)
+    jobs = [Gather(me, bw_ref, send, recv, 0)]
+    jobs += [Gather(me, jw_ref.at[u], send, recv, 1 + u) for u in range(3)]
+    jobs += [Gather(me, mix_ref, send, recv, 4)]
+    jobs += [Gather(me, early_ref.at[u], send, recv, 5 + u) for u in range(early)]
+    events = []
+    for u, job in enumerate(jobs):
+        for k, when in enumerate(GATHER_TICKS):
+            events.append((2 * u + when, k, u, (job.start, job.step1, job.step2, job.step3, job.step4)[k]))
+    events.sort(key=lambda e: (e[0], -e[1]))
+    n_early = 4
+    for event in events[:n_early]:
+        event[3]()
+    rows = jnp.concatenate([lift_ref[:, u * 512 : (u + 1) * 512] for u in range(nf)], axis=0)
+    rows = mm(rows, unit_order()).astype(BF)
+    for f in range(early // 2):
+        lift = jnp.concatenate([rows[16 * u : 16 * u + 16, 128 * f : 128 * f + 128] for u in range(nf)], axis=1)
+        drop = drop_ref[16 * f : 16 * f + 16, :]
+        early_ref[(2 * f,) + here] = lift
+        early_ref[(2 * f + 1,) + here] = drop
+    seg = seg_ref[...]
+    lane = lax.broadcasted_iota(jnp.int32, starts_ref.shape, 1)
+    starts = jnp.zeros(starts_ref.shape, jnp.int32)
+    for v in range(1, 6):
+        count = jnp.sum(jnp.where(seg < v, 1.0, 0.0), axis=1, keepdims=True).astype(jnp.int32)
+        starts = jnp.where(lane == v, count, starts)
+    starts_ref[...] = starts
+
+    for _, k, u, run in events[n_early:]:
+        run()
+        if k < 4:
+            continue
+        u -= 1
+        if u < 0:
+            bias_ref[...] = bw_ref[...].reshape(512, 128).astype(F32).T[:8]
+        elif u < 3:
+
+            @pl.loop(0, tokens // 512)
+            def _(b, u=u):
+                rows = pl.ds(pl.multiple_of(b * 512, 512), 512)
+                y = mm(tok_ref[rows, :], jw_ref[u].reshape(512, 512))
+                if u == 0:
+                    y = y + bias_ref[6:7, :]
+                if u == 2:
+                    y = y + bias_ref[7:8, :]
+                qkv_ref[rows, u * 512 : (u + 1) * 512] = y.astype(BF)
 
     for job in jobs:
         job.finish()
 
 
-def first(nz, tok, own, bias_own):
-    units = own.shape[0]
+def first(nz, tok, joint, mix, lift, drop, bias_own, seg):
     tokens = tok.shape[0]
     vmem = pl.BlockSpec(memory_space=pltpu.VMEM)
+    unit = (nz, 2, 2, 2, 16, 512)
     return pl.pallas_call(
         functools.partial(first_kernel, nz),
-        in_specs=[vmem] * 3,
-        out_specs=[vmem] * 3,
+        in_specs=[vmem] * 7,
+        out_specs=[vmem] * 6,
         out_shape=[
             jax.ShapeDtypeStruct((tokens, 1536), BF),
-            jax.ShapeDtypeStruct((units, nz, 2, 2, 2, 16, 512), BF),
+            jax.ShapeDtypeStruct((3,) + unit, BF),
+            jax.ShapeDtypeStruct(unit, BF),
+            jax.ShapeDtypeStruct((EARLY,) + unit, BF),
             jax.ShapeDtypeStruct((8, 512), F32),
+            jax.ShapeDtypeStruct((seg.shape[0], 128), jnp.int32),
         ],
-        scratch_shapes=[pltpu.VMEM((1, nz, 2, 2, 2, 16, 128), BF)] + sems(units, nz) + sems(1, nz),
+        scratch_shapes=[pltpu.VMEM((nz, 2, 2, 2, 16, 128), BF)] + sems(5 + EARLY, nz),
         compiler_params=pltpu.CompilerParams(vmem_limit_bytes=VMEM_LIMIT, collective_id=1, has_side_effects=True),
         name="gather_joint",
-    )(tok, own, bias_own)
+    )(tok, joint, mix, lift, drop, bias_own, seg)
 
 
 def middle_kernel(
@@ -627,13 +705,14 @@
     cot_ref,
     mix_ref,
     early_ref,
-    own_ref,
+    late_ref,
     bias_ref,
     out_ref,
     gmid_ref,
     gctx_ref,
     gmix_ref,
     gbias_ref,
+    kept_ref,
     grad_ref,
     w_ref,
     hid_ref,
@@ -644,9 +723,7 @@
     gl_ref,
     gdt_ref,
     sum_ref,
-    early_sem,
-    gsend,
-    grecv,
+    load_sem,
     rsend,
     rrecv,
     *bufs,
@@ -656,22 +733,18 @@
     nf = w_ref.shape[0] // 2
     nb = tokens // tb
     early = early_ref.shape[0]
-    load = pltpu.make_async_copy(early_ref, w_ref.at[0:early], early_sem)
-    load.start()
+    loads = [pltpu.make_async_copy(early_ref, w_ref.at[0:early], load_sem.at[0])]
+    for u in range(early, 2 * nf):
+        at = (u - early) * 512
+        loads.append(pltpu.make_async_copy(late_ref.at[:, at : at + 512], w_ref.at[u], load_sem.at[u]))
+    for load in loads:
+        load.start()
     ones = jnp.ones((16, tb), BF)
-
-    def gathers(f):
-        return [Gather(me, w_ref.at[2 * f + i], gsend, grecv, 2 * f + i) for i in range(2)]
 
     def reduces(f):
         return [Reduce(me, bufs, 2 * f + i, rsend, rrecv) for i in range(2)]
 
-    for u in range(early, 2 * nf):
-        w_ref[u, me.z, me.y, me.x, me.c] = own_ref[u - early]
     me.greet()
-    for f in range(early // 2, nf):
-        for job in gathers(f):
-            job.start()
 
     @pl.loop(0, nb)
     def _(b):
@@ -687,18 +760,13 @@
         gmid_ref[rows, :] = c.astype(F32)
 
     gbias_ref[...] = jnp.zeros_like(gbias_ref)
-    load.wait()
-
-    def lift(f):
-        return w_ref.at[2 * f]
-
-    def drop(f):
-        return w_ref.at[2 * f + 1]
+    for load in loads:
+        load.wait()
 
     def stage1(f, b):
         rows = pl.ds(b * tb, tb)
-        lw = w_ref[2 * f].reshape(512, 512)
-        dw = w_ref[2 * f + 1].reshape(512, 512)
+        lw = w_ref[2 * f]
+        dw = w_ref[2 * f + 1]
         for n in range(0, 512, 256):
             x = mm(hid_ref[rows, :], lw[:, n : n + 256]) + bias_ref[pl.ds(f, 1), n : n + 256]
             grad = mm(cot_ref[rows, :], dw[n : n + 256, :], NT)
@@ -711,8 +779,8 @@
         rows = pl.ds(b * tb, tb)
         act = act_ref[b]
         gl = gl_ref[b]
-        acc_ref[rows, :] += mm(act, w_ref[2 * f + 1].reshape(512, 512))
-        gmid_ref[rows, :] += mm(gl, w_ref[2 * f].reshape(512, 512), NT)
+        acc_ref[rows, :] += mm(act, w_ref[2 * f + 1])
+        gmid_ref[rows, :] += mm(gl, w_ref[2 * f], NT)
         gd = mm(cott_ref[:, rows], act)
         gf = mm(hidt_ref[:, rows], gl)
         unit = gf[:width].reshape(nz, 2, 2, 2, 16, 512)
@@ -741,10 +809,6 @@
             else:
                 grad_ref[2 * f + i] = job.step4()
 
-    def gather_step(f, k):
-        for job in gathers(f):
-            (job.step1, job.step2, job.step3, job.step4)[k]()
-
     @pl.loop(0, nf)
     def _(f):
         for k in range(nb):
@@ -752,18 +816,17 @@
             @pl.when(f > 0)
             def _(k=k):
                 if k == 0:
-                    gather_step(f, 3)
-                reduce_step(f - 1, k)
-
-            @pl.when(f + 1 < nf)
+                    reduce_step(f - 1, 0)
+                if k == 1:
+                    reduce_step(f - 1, 1)
+                if k == 3:
+                    reduce_step(f - 1, 2)
+
+            @pl.when(f > 1)
             def _(k=k):
-                if k < 3:
-                    gather_step(f + 1, k)
-
-            if k == 0:
-
-                @pl.when(f > 1)
-                def _():
+                if k == 1:
+                    reduce_step(f - 2, 3)
+                if k == 3:
                     reduce_step(f - 2, 4)
 
             stage1(f, k)
@@ -773,9 +836,8 @@
 
     gmix_ref[...] = jnp.zeros_like(gmix_ref)
     for b in range(nb):
-        if b == 0:
-            reduce_step(nf - 2, 4)
-        reduce_step(nf - 1, b)
+        if b == 1:
+            reduce_step(nf - 2, 3)
         rows = pl.ds(b * tb, tb)
         out_ref[rows, :] = acc_ref[rows, :].astype(BF)
         gb = gmid_ref[rows, :].astype(BF)
@@ -783,34 +845,33 @@
         gmix_ref[...] += mm(ctx_ref[rows, :].T, gb)
         gbias_ref[5:6, :] += mm(ones, gb)[0:1]
         gbias_ref[4:5, :] += mm(ones, cot_ref[rows, :])[0:1]
-    reduce_step(nf - 1, 4)
-    for f in range(nf):
-        if f >= early // 2:
-            for job in gathers(f):
-                job.finish()
+    kept_ref[...] = sum_ref[(nf - 1) % 2]
+    reduce_step(nf - 2, 4)
+    for f in range(nf - 1):
         for job in reduces(f):
             job.finish()
 
 
-def middle(nz, tok, ctx, cot, mix, early, own, bias):
+def middle(nz, tok, ctx, cot, mix, early, late, bias):
     tokens, width = tok.shape
-    n = early.shape[0] + own.shape[0]
+    n = early.shape[0] + late.shape[1] // 512
     tb = tokens // 4
     vmem = pl.BlockSpec(memory_space=pltpu.VMEM)
     return pl.pallas_call(
         functools.partial(middle_kernel, nz, tb),
-        in_specs=[vmem] * 4 + [pl.BlockSpec(memory_space=pl.ANY)] + [vmem] * 2,
-        out_specs=[vmem] * 6,
+        in_specs=[vmem] * 4 + [pl.BlockSpec(memory_space=pl.ANY)] * 2 + [vmem],
+        out_specs=[vmem] * 7,
         out_shape=[
             jax.ShapeDtypeStruct((tokens, width), BF),
             jax.ShapeDtypeStruct((tokens, width), F32),
             jax.ShapeDtypeStruct((tokens, width), BF),
             jax.ShapeDtypeStruct((width, width), F32),
             jax.ShapeDtypeStruct((8, 512), F32),
-            jax.ShapeDtypeStruct((n, 16, 512), F32),
+            jax.ShapeDtypeStruct((2, nz, 2, 2, 2, 16, 512), F32),
+            jax.ShapeDtypeStruct((n - 2, 16, 512), F32),
         ],
         scratch_shapes=[
-            pltpu.VMEM((n, nz, 2, 2, 2, 16, 512), BF),
+            pltpu.VMEM((n, 512, 512), BF),
             pltpu.VMEM((tokens, width), BF),
             pltpu.VMEM((width + 16, tokens), BF),
             pltpu.VMEM((width, tokens), BF),
@@ -819,27 +880,28 @@
             pltpu.VMEM((4, tb, 512), BF),
             pltpu.VMEM((width, 512), F32),
             pltpu.VMEM((2, 2, nz, 2, 2, 2, 16, 512), F32),
-            pltpu.SemaphoreType.DMA,
+            pltpu.SemaphoreType.DMA((n,)),
         ]
-        + sems(n, nz)
-        + sems(n, nz)
-        + reduce_bufs(n, nz, 512),
+        + sems(n - 2, nz)
+        + reduce_bufs(n - 2, nz, 512),
         compiler_params=pltpu.CompilerParams(vmem_limit_bytes=VMEM_LIMIT, collective_id=2, has_side_effects=True),
         name="feed",
-    )(tok, ctx, cot, mix, early, own, bias)
+    )(tok, ctx, cot, mix, early, late, bias)
 
 
 def last_kernel(
     nz,
     tok_ref,
     gj_ref,
-    gmid_ref,
-    jw_ref,
     gmix_ref,
     gbias_ref,
-    tg_ref,
-    own_ref,
+    kept_ref,
+    grad_ref,
+    joint_ref,
+    mix_ref,
     obias_ref,
+    glift_ref,
+    gdrop_ref,
     tokt_ref,
     sum_ref,
     bsum_ref,
@@ -852,72 +914,102 @@
 ):
     me = Place(nz)
     tokens, width = tok_ref.shape
+    n = 7
+    nf = glift_ref.shape[1] // 512
     me.greet()
-    jobs = [Reduce(me, bufs[:9], u, send, recv) for u in range(4)] + [Reduce(me, bufs[9:], 0, bsend, brecv)]
-    units = [gmix_ref] + [sum_ref.at[j] for j in range(3)] + [bsum_ref]
-    n = 5
-    jobs[0].start(units[0])
-
-    @pl.loop(0, tokens // 512)
-    def _(b):
-        rows = pl.ds(pl.multiple_of(b * 512, 512), 512)
-        tokt_ref[0:width, rows] = tok_ref[rows, :].T
-        tokt_ref[width : width + 16, rows] = jnp.ones((16, 512), BF)
-
-    def token_block(b):
-        rows = pl.ds(pl.multiple_of(b * 512, 512), 512)
-        total = gmid_ref[rows, :]
-        for j in range(3):
-            total = total + mm(gj_ref[rows, j * 512 : (j + 1) * 512], jw_ref[j], NT)
-        tg_ref[rows, :] = total
-
-    brow_ref[...] = jnp.zeros_like(brow_ref)
-    brow_ref[0:8, :] = gbias_ref[...]
-    done = 0
-    for s in range(n + 4):
-        if 0 <= s - 4 < n:
-            u = s - 4
-            total = jobs[u].step4()
-            if u < 4:
-                own_ref[u] = total
-            else:
-                obias_ref[...] = total
-        if 0 <= s - 3 < n:
-            jobs[s - 3].step3()
-        if 0 <= s - 2 < n:
-            jobs[s - 2].step2()
-        if 0 <= s - 1 < n:
-            jobs[s - 1].step1(units[s - 1])
-        if s < 3:
-            g = mm(tokt_ref[...], gj_ref[:, s * 512 : (s + 1) * 512])
-            sum_ref[s] = g[:width].reshape(nz, 2, 2, 2, 16, 512)
-            if s != 1:
-                brow_ref[6 + s // 2 : 7 + s // 2, :] = g[width : width + 1]
-            jobs[s + 1].start(units[s + 1])
-        elif s == 3:
+    jobs = [Reduce(me, bufs[:9], u, send, recv) for u in range(n - 1)] + [Reduce(me, bufs[9:], 0, bsend, brecv)]
+    units = [kept_ref.at[0], kept_ref.at[1], gmix_ref] + [sum_ref.at[j] for j in range(3)] + [bsum_ref]
+
+    def begin(u):
+        if u == n - 1:
             bsum_ref[...] = brow_ref[...].T.reshape(nz, 2, 2, 2, 16, 128)
-            jobs[4].start(units[4])
-        if s >= 3 and done < tokens // 512:
-            token_block(done)
-            done += 1
-    while done < tokens // 512:
-        token_block(done)
-        done += 1
+        elif u > 2:
+            if u == 3:
+
+                @pl.loop(0, tokens // 512)
+                def _(b):
+                    rows = pl.ds(pl.multiple_of(b * 512, 512), 512)
+                    tokt_ref[0:width, rows] = tok_ref[rows, :].T
+                    tokt_ref[width : width + 16, rows] = jnp.ones((16, 512), BF)
+
+                brow_ref[...] = jnp.zeros_like(brow_ref)
+                brow_ref[0:8, :] = gbias_ref[...]
+            g = mm(tokt_ref[...], gj_ref[:, (u - 3) * 512 : (u - 2) * 512])
+            sum_ref[u - 3] = g[:width].reshape(nz, 2, 2, 2, 16, 512)
+            if u != 4:
+                at = 6 + (u - 3) // 2
+                brow_ref[at : at + 1, :] = g[width : width + 1]
+        jobs[u].start(units[u])
+
+    def put_lift(last):
+        g = jnp.concatenate(
+            [
+                jnp.concatenate(
+                    [grad_ref[2 * f, :, 128 * u : 128 * u + 128] for f in range(nf - 1)]
+                    + [last[:, 128 * u : 128 * u + 128]],
+                    axis=1,
+                )
+                for u in range(nf)
+            ],
+            axis=0,
+        )
+        order = unit_order()
+        high = g.astype(BF)
+        rest = g - high.astype(F32)
+        part = rest.astype(BF)
+        low = (rest - part.astype(F32)).astype(BF)
+        g = mm(high, order, NT) + mm(part, order, NT) + mm(low, order, NT)
+        for u in range(nf):
+            glift_ref[:, 512 * u : 512 * u + 512] = g[16 * u : 16 * u + 16]
+
+    def end(u):
+        total = jobs[u].step4()
+        if u == 0:
+            put_lift(total)
+        elif u == 1:
+            for f in range(nf - 1):
+                gdrop_ref[16 * f : 16 * f + 16, :] = grad_ref[2 * f + 1]
+            gdrop_ref[16 * nf - 16 : 16 * nf, :] = total
+        elif u == 2:
+            mix_ref[...] = total
+        elif u < n - 1:
+            joint_ref[:, (u - 3) * 512 : (u - 2) * 512] = total
+        else:
+            obias_ref[...] = total.T
+
+    def run(u, k):
+        if k == 0:
+            begin(u)
+        elif k == 1:
+            jobs[u].step1(units[u])
+        elif k == 2:
+            jobs[u].step2()
+        elif k == 3:
+            jobs[u].step3()
+        else:
+            end(u)
+
+    events = [(2 * u + when, k, u) for u in range(n) for k, when in enumerate(REDUCE_TICKS)]
+    for _, k, u in sorted(events, key=lambda e: (e[0], -e[1])):
+        run(u, k)
     for job in jobs:
         job.finish()
 
 
-def last(nz, tok, gj, gmid, jw, gmix, gbias):
+def last(nz, tok, gj, gmix, gbias, kept, grads):
     tokens, width = tok.shape
+    n = grads.shape[0] + 2
     vmem = pl.BlockSpec(memory_space=pltpu.VMEM)
     return pl.pallas_call(
         functools.partial(last_kernel, nz),
         in_specs=[vmem] * 6,
-        out_specs=[vmem] * 3,
+        out_specs=[vmem] * 5,
         out_shape=[
-            jax.ShapeDtypeStruct((tokens, width), F32),
-            jax.ShapeDtypeStruct((4, 16, 512), F32),
-            jax.ShapeDtypeStruct((16, 128), F32),
+            jax.ShapeDtypeStruct((16, 1536), F32),
+            jax.ShapeDtypeStruct((16, 512), F32),
+            jax.ShapeDtypeStruct((128, 16), F32),
+            jax.ShapeDtypeStruct((16, n // 2 * 512), F32),
+            jax.ShapeDtypeStruct((n // 2 * 16, 512), F32),
         ],
         scratch_shapes=[
             pltpu.VMEM((width + 16, tokens), BF),
@@ -925,16 +1017,13 @@
             pltpu.VMEM((nz, 2, 2, 2, 16, 128), F32),
             pltpu.VMEM((128, 512), F32),
         ]
-        + sems(4, nz)
+        + sems(6, nz)
         + sems(1, nz)
-        + reduce_bufs(4, nz, 512)
+        + reduce_bufs(6, nz, 512)
         + reduce_bufs(1, nz, 128),
         compiler_params=pltpu.CompilerParams(vmem_limit_bytes=VMEM_LIMIT, collective_id=3, has_side_effects=True),
         name="joint_grads",
-    )(tok, gj, gmid, jw, gmix.reshape(nz, 2, 2, 2, 16, 512), gbias)
-
-
-EARLY = 2
+    )(tok, gj, gmix.reshape(nz, 2, 2, 2, 16, 512), gbias, kept, grads)
 
 
 def remote_body(
@@ -955,46 +1044,36 @@
     nz = lax.axis_size("gx")
     n_tok = rows * length
     tok = tokens.reshape(n_tok, width)
-    cot = cotangent.reshape(n_tok, width)
-    seg = segment_ids.reshape(rows, 1, length)
-    starts = jnp.sum(
-        segment_ids[:, None, :] < jnp.arange(8, dtype=jnp.int32)[None, :, None], axis=-1, dtype=jnp.int32
-    )
     nf = drop_weight.shape[0] // 16
-    lift_own = lift_weight.reshape(16, -1, nf, 16).transpose(2, 0, 1, 3).reshape(nf, 16, 512)
-    drop_own = drop_weight.reshape(nf, 16, 512)
-    joint_own = joint_weight.reshape(16, 3, 512).transpose(1, 0, 2)
-    feed_own = jnp.stack([lift_own, drop_own], axis=1).reshape(2 * nf, 16, 512)
-    first_own = jnp.concatenate([joint_own, mix_weight[None], feed_own[:EARLY]])
     bias_own = jnp.concatenate([lift_bias.reshape(nf, 16), drop_bias[None], mix_bias[None], joint_bias])
     bias_own = jnp.pad(bias_own, ((0, 120), (0, 0))).T
-
-    qkv, weights, bias = first(nz, tok, first_own, bias_own)
+    lift_own = lift_weight.reshape(16, -1, nf, 16)
+    late = []
+    for f in range(EARLY // 2, nf):
+        late += [lift_own[:, :, f].reshape(16, 512), drop_weight[16 * f : 16 * f + 16]]
+    late = lax.all_gather(jnp.concatenate(late, axis=1), BOTH, axis=0, tiled=True)
+    qkv, joint_w, mix_w, early, bias, starts = first(
+        nz, tok, joint_weight, mix_weight, lift_weight, drop_weight, bias_own, segment_ids
+    )
     qkv3 = qkv.reshape(rows, length, 3 * width)
-    ctx, lse = attend(starts, fill_lengths, seg, qkv3)
-    out, gmid, gctx, gmix, gbias, feed_grads = middle(
-        nz, tok, ctx.reshape(n_tok, width), cot, weights[3].reshape(width, width), weights[4:], feed_own[EARLY:], bias
+    ctx, lse = attend(starts, fill_lengths, segment_ids, qkv3)
+    out, gmid, gctx, gmix, gbias, kept, grads = middle(
+        nz, tok, ctx.reshape(n_tok, width), cotangent.reshape(n_tok, width), mix_w.reshape(width, width), early.reshape(EARLY, 512, 512), late, bias
     )
-    gjoint = attend_back(
-        starts, fill_lengths, seg, qkv3, lse, ctx, gctx.reshape(rows, length, width)
-    ).reshape(n_tok, 3 * width)
-    token_grad, grads, gb = last(nz, tok, gjoint, gmid, weights[:3].reshape(3, width, width), gmix, gbias)
-    feed_grads = feed_grads.reshape(nf, 2, 16, 512)
-    glift = feed_grads[:, 0].reshape(nf, 16, -1, 16).transpose(1, 2, 0, 3).reshape(16, nf * 512)
-    gdrop = feed_grads[:, 1].reshape(nf * 16, 512)
-    gb = gb[:, :8].T
-    return (
+    gjoint, token_grad, out = attend_back(
+        starts,
+        fill_lengths,
+        segment_ids,
+        qkv3,
+        lse,
+        ctx,
+        gctx.reshape(rows, length, width),
+        gmid.reshape(rows, length, width),
+        joint_w.reshape(3, width, width),
         out.reshape(rows, length, width),
-        token_grad.reshape(rows, length, width),
-        grads[1:4].transpose(1, 0, 2).reshape(16, 3 * width),
-        gb[6:8],
-        grads[0],
-        gb[5],
-        glift,
-        gb[:nf].reshape(-1),
-        gdrop,
-        gb[4],
     )
+    gj, gm, gb, glift, gdrop = last(nz, tok, gjoint.reshape(n_tok, 3 * width), gmix, gbias, kept, grads)
+    return (out, token_grad, gj, gb[6:8], gm, gb[5], glift, gb[:nf].reshape(-1), gdrop, gb[4])
 
 
 BOTH = ("gx", "gy")
@@ -1018,9 +1097,8 @@
     n_tok = rows * length
     tok = tokens.reshape(n_tok, width)
     cot = cotangent.reshape(n_tok, width)
-    seg = segment_ids.reshape(rows, 1, length)
     starts = jnp.sum(
-        segment_ids[:, None, :] < jnp.arange(8, dtype=jnp.int32)[None, :, None], axis=-1, dtype=jnp.int32
+        segment_ids[:, None, :] < jnp.arange(128, dtype=jnp.int32)[None, :, None], axis=-1, dtype=jnp.int32
     )
 
     joint_w = lax.all_gather(joint_weight, BOTH, axis=0, tiled=True)
@@ -1043,17 +1121,26 @@
     shift = jnp.concatenate([bq, jnp.zeros_like(bq), bv])
     qkv = (mm(tok, joint_w) + shift).astype(BF)
     qkv3 = qkv.reshape(rows, length, 3 * width)
-    ctx, lse = attend(starts, fill_lengths, seg, qkv3)
+    ctx, lse = attend(starts, fill_lengths, segment_ids, qkv3)
     lift_units = lift_w.reshape(width, nf, 512).transpose(1, 0, 2)
     out, gmid, gctx, glift, gdrop, gmix, gbias = feed(
         tok, ctx.reshape(n_tok, width), cot, mix_w, lift_units, drop_w.reshape(nf, 512, width), bias
     )
-    gjoint = attend_back(
-        starts, fill_lengths, seg, qkv3, lse, ctx, gctx.reshape(rows, length, width)
-    ).reshape(n_tok, 3 * width)
+    gjoint, token_grad, out = attend_back(
+        starts,
+        fill_lengths,
+        segment_ids,
+        qkv3,
+        lse,
+        ctx,
+        gctx.reshape(rows, length, width),
+        gmid.reshape(rows, length, width),
+        joint_w.reshape(width, 3, width).transpose(1, 0, 2),
+        out.reshape(rows, length, width),
+    )
+    gjoint = gjoint.reshape(n_tok, 3 * width)
     gjoint_w = lax.dot_general(tok, gjoint, (((0,), (0,)), ((), ())), preferred_element_type=F32)
     sums = jnp.sum(gjoint.astype(F32), axis=0)
-    token_grad = gmid + mm(gjoint, joint_w, NT)
 
     glift_w = glift[:, :width].transpose(1, 0, 2).reshape(width, nf * 512)
     gdrop_w = gdrop.transpose(0, 2, 1).reshape(nf * 512, width)
@@ -1072,8 +1159,8 @@
         cuts.append(own[at : at + size])
         at += size
     return (
-        out.reshape(rows, length, width),
-        token_grad.reshape(rows, length, width),
+        out,
+        token_grad,
         scatter(gjoint_w),
         jnp.stack([cuts[0], cuts[1]]),
         scatter(gmix),

time: 265 us -> 229 us (0.86)
  Pallas kernels: 232 us -> 194 us
  between operations: 1 us -> 14.3 us
  local copies, waits for them, and re-layouts: 27.1 us -> 16.9 us
    pallas_call x1, Pallas kernels: 92.4 us -> 59.1 us  [middle(): pl.pallas_call(functools.partial(middle_kernel, nz, tb), in_specs=[vmem]...]
    pallas_call x1, Pallas kernels: 44.8 us -> 36.3 us  [last(): pl.pallas_call(functools.partial(last_kernel, nz), in_specs=[vmem] * 6, o...]
    slice x5 -> x2, local copies, waits for them, and re-layouts: 7 us -> 2.39 us  [the longest x1 1.65 us: remote_body(): lift_own[:, :, f].reshape(16, 512)]
    reshape x4 -> x1, local copies, waits for them, and re-layouts: 4.28 us -> 1.24 us  [remote_body(): lift_own = lift_weight.reshape(16, -1, nf, 16)]
    pallas_call x1, Pallas kernels: 38 us -> 40.8 us  [first(): pl.pallas_call(functools.partial(first_kernel, nz), in_specs=[vmem] * 7,...]
    unnamed x15 -> x5, local copies, waits for them, and re-layouts: 7.52 us -> 6.79 us
  transfers between devices with their start and end apart: 0 -> 1, of which waited for: 0 -> 0; matrix products, arithmetic and copies ran while one was open for 0% -> 2% of each run, Pallas kernels for 0% -> 28%
where the time goes in v3:
time: 229 us; the launch traced here: 226 us
  Pallas kernels  194 us (85%)
  local copies, waits for them, and re-layouts  16.9 us (7%)
  between operations  14.3 us (6%)
    pallas_call x1, Pallas kernels, middle(): pl.pallas_call(functools.partial(middle_kernel, nz, tb), in_specs=[vmem]...  59.1 us
    pallas_call x1, Pallas kernels, first(): pl.pallas_call(functools.partial(first_kernel, nz), in_specs=[vmem] * 7,...  40.8 us
    pallas_call x1, Pallas kernels, last(): pl.pallas_call(functools.partial(last_kernel, nz), in_specs=[vmem] * 6, o...  36.3 us
    pallas_call x1, Pallas kernels, attend_back(): pl.pallas_call(functools.partial(attend_back_kernel, length=length), grid...  35.6 us
    pallas_call x1, Pallas kernels, attend(): pl.pallas_call(functools.partial(attend_kernel, length=length), grid_spec...  21.9 us
    unnamed x5, local copies, waits for them, and re-layouts  6.79 us
  transfers between devices with their start and end apart: 1, of which 0 were waited for; matrix products, arithmetic and copies ran while one was open for 2% of the time, Pallas kernels for 28%

profile of v3, /device:TPU:0, one launch (start us, length us, event | category | flops | bytes accessed | tf_op | source)
XLA Modules:
  0.0 226.3 jit_solution(16496010293176290508)
XLA Ops:
  7.2 0.0 all-gather.2.cloned.1.call-start
  7.2 0.7 fusion.8
  8.0 1.2 reshape.72
  9.2 1.7 slice_reduce_fusion.1
  10.9 0.2 reshape_squeeze.6
  11.1 0.2 reshape_squeeze.7
  11.2 0.6 pad_maximum_fusion
  11.9 0.0 all-gather.2.cloned.1.call-update
  11.9 0.7 reshape.66
  12.6 0.1 copy.28
  12.7 0.7 copy.31
  13.5 0.7 copy.30
  14.2 0.7 copy.29
  15.0 0.7 fusion.7.bias_own_ref
  15.7 40.8 %gather_joint.1 = (bf16[2048,1536]{1,0:T(8,128)(2,1)}, bf16[3,4,2,2,2,16,512]{6,5,4,3,2,1,0:T(8,128)(2,1)}, bf16[4,2,2,2,16,512]{5,4,3,2,1,0:T(8,128)(2,1)}, bf1...) custom-call(bf16[2048,512]{1,0:T(8,128)(2,1)} %bitcast.22, ...), custom_call_target="tpu_custom_call" | custom-call | tf_op jit(solution)/shard_map/gather_joint/pallas_call | solution.py:682
  56.5 21.9 %attend.1 = (bf16[2,1024,512]{2,1,0:T(8,128)(2,1)}, f32[2,4,8,256]{3,2,1,0:T(8,128)}) custom-call(s32[2,128]{1,0:T(2,128)} %get-tuple-element.33.starts_ref, s32[2]{0:T(128)} %fill_ref.3, s32[2,1024]{1,0:T(2,128)} %seg_ref.5, bf16[2,1024,1536]{2,1,0:T(8,128)(2,1)} %bitcast.20), custom_call_target="tpu_custom_call" | custom-call | tf_op jit(solution)/shard_map/attend/pallas_call | solution.py:134
  78.4 0.0 all-gather.2.cloned.1.call-done.late_ref
  78.4 59.1 %feed.1 = (bf16[2048,512]{1,0:T(8,128)(2,1)}, f32[2048,512]{1,0:T(8,128)}, bf16[2048,512]{1,0:T(8,128)(2,1)}, f32[512,512]{1,0:T(8,128)}, f32[8,512]{1,0:T(8,128...) custom-call(bf16[2048,512]{1,0:T(8,128)(2,1)} %bitcast.23, bf16[2048,512]{1,0:T(8,128)(2,1)} %bitcast.25, ...), custom_call_target="tpu_custom_call" | custom-call | tf_op jit(solution)/shard_map/feed/pallas_call | solution.py:860
  137.5 35.6 %attend_back.1 = (bf16[2,1024,1536]{2,1,0:T(8,128)(2,1)}, f32[2,1024,512]{2,1,0:T(8,128)}, bf16[2,1024,512]{2,1,0:T(8,128)(2,1)}) custom-call(s32[2,128]{1,0:T(2,128)} %get-tuple-element.33.starts_ref, s32[2]{0:T(128)} %fill_ref.3, s32[2,1024]{1,0:T(2,128)} %seg_ref.5, bf16[2,1024,1536]{2,1,0:T(8,128)(2,1)} %bitcast.21, ...), custom_call_target="tpu_custom_call" | custom-call | tf_op jit(solution)/shard_map/attend_back/pallas_call | solution.py:259
  173.1 36.3 %joint_grads.1 = (f32[16,1536]{1,0:T(8,128)}, f32[16,512]{1,0:T(8,128)}, f32[128,16]{1,0:T(8,128)}, f32[16,2048]{1,0:T(8,128)}, f32[64,512]{1,0:T(8,128)}) custom-call(bf16[2048,512]{1,0:T(8,128)(2,1)} %bitcast.24, bf16[2048,1536]{1,0:T(8,128)(2,1)} %bitcast.26, f32[4,2,2,2,16,512]{5,4,3,2,1,0:T(8,128)} %bitcast.33, f32[8,512]{1,0:T(8,128)} %get-tuple-element.48.gbias_ref, ...), custom_call_target="tpu_custom_call" | custom-call | tf_op jit(solution)/shard_map/joint_grads/pallas_call | solution.py:1003
  209.4 1.2 slice.28
  210.7 1.3 slice_bitcast_fusion
  212.0 0.7 slice.30
  212.7 0.6 reshape.79
  213.2 1.5 copy.36
  214.8 1.4 copy.37
  216.2 1.6 copy.38
  217.7 1.6 copy.39
Async XLA Ops:
  7.2 71.2 %all-gather.2.cloned.1.call-start = ((), (), s32[]{:S(2)}) async-start(), calls=%async_computation | async-start | bytes 2162688 | tf_op jit(solution)/shard_map/all_gather | solution.py:1054
Sparse Core Ops, SparseCore 0:
  12.0 60.2 all-gather.1

commit v4 on v3

--- a/solution.py
+++ b/solution.py
@@ -425,6 +425,8 @@
 MESH = pl.DeviceIdType.MESH
 GATHER_TICKS = (0, 6, 10, 14, 16)
 REDUCE_TICKS = (0, 3, 8, 13, 17)
+GATHER_AT = ((1, 1), (3, 2), (6, 3), (8, 4))
+REDUCE_AT = (0, 2, 5, 7, 9)
 EARLY = 4
 
 
@@ -598,29 +600,52 @@
 
 def first_kernel(
     nz,
-    tok_ref,
+    tok_hbm,
     joint_ref,
     mix_own_ref,
     lift_ref,
     drop_ref,
-    bias_own_ref,
+    bl_ref,
+    bd_ref,
+    bm_ref,
+    bj_ref,
     seg_ref,
+    qkv_hbm,
+    jw_hbm,
+    mix_hbm,
+    early_hbm,
+    late_own_ref,
+    bias_ref,
+    starts_ref,
+    tok_ref,
     qkv_ref,
     jw_ref,
     mix_ref,
     early_ref,
-    bias_ref,
-    starts_ref,
     bw_ref,
+    line_ref,
+    tok_sem,
+    qkv_sem,
+    unit_sem,
     send,
     recv,
 ):
     me = Place(nz)
+    load = pltpu.make_async_copy(tok_hbm, tok_ref, tok_sem)
+    load.start()
     tokens, width = tok_ref.shape
     early = early_ref.shape[0]
     nf = drop_ref.shape[0] // 16
     here = (me.z, me.y, me.x, me.c)
-    bw_ref[here] = bias_own_ref[...]
+    line_ref[...] = jnp.zeros_like(line_ref)
+    line_ref[0:1, 0 : 16 * nf] = bl_ref[...].astype(F32)
+    line_ref[4:5, 0:16] = bd_ref[...].astype(F32)
+    line_ref[5:6, 0:16] = bm_ref[...].astype(F32)
+    line_ref[6:8, 0:16] = bj_ref[...].astype(F32)
+    lift_line = line_ref[0:1, :]
+    for f in range(1, nf):
+        line_ref[f : f + 1, :] = pltpu.roll(lift_line, 128 - 16 * f, 1)
+    bw_ref[here] = line_ref[...].T[:16].astype(BF)
     for u in range(3):
         jw_ref[(u,) + here] = joint_ref[:, u * 512 : (u + 1) * 512]
     mix_ref[here] = mix_own_ref[...]
@@ -639,11 +664,15 @@
         event[3]()
     rows = jnp.concatenate([lift_ref[:, u * 512 : (u + 1) * 512] for u in range(nf)], axis=0)
     rows = mm(rows, unit_order()).astype(BF)
-    for f in range(early // 2):
+    for f in range(nf):
         lift = jnp.concatenate([rows[16 * u : 16 * u + 16, 128 * f : 128 * f + 128] for u in range(nf)], axis=1)
         drop = drop_ref[16 * f : 16 * f + 16, :]
-        early_ref[(2 * f,) + here] = lift
-        early_ref[(2 * f + 1,) + here] = drop
+        if 2 * f < early:
+            early_ref[(2 * f,) + here] = lift
+            early_ref[(2 * f + 1,) + here] = drop
+        else:
+            late_own_ref[2 * f - early] = lift
+            late_own_ref[2 * f - early + 1] = drop
     seg = seg_ref[...]
     lane = lax.broadcasted_iota(jnp.int32, starts_ref.shape, 1)
     starts = jnp.zeros(starts_ref.shape, jnp.int32)
@@ -652,12 +681,21 @@
         starts = jnp.where(lane == v, count, starts)
     starts_ref[...] = starts
 
+    gathered = [(jw_ref.at[u], jw_hbm.at[u]) for u in range(3)] + [(mix_ref, mix_hbm)]
+    gathered += [(early_ref.at[u], early_hbm.at[u]) for u in range(early)]
+    stores = [pltpu.make_async_copy(a, b, unit_sem.at[i]) for i, (a, b) in enumerate(gathered)]
+    for u in range(3):
+        columns = slice(u * 512, (u + 1) * 512)
+        stores.append(pltpu.make_async_copy(qkv_ref.at[:, columns], qkv_hbm.at[:, columns], qkv_sem.at[u]))
     for _, k, u, run in events[n_early:]:
         run()
         if k < 4:
             continue
         u -= 1
+        if u >= 0:
+            stores[u].start()
         if u < 0:
+            load.wait()
             bias_ref[...] = bw_ref[...].reshape(512, 128).astype(F32).T[:8]
         elif u < 3:
 
@@ -671,49 +709,76 @@
                     y = y + bias_ref[7:8, :]
                 qkv_ref[rows, u * 512 : (u + 1) * 512] = y.astype(BF)
 
+            stores[len(gathered) + u].start()
+
     for job in jobs:
         job.finish()
-
-
-def first(nz, tok, joint, mix, lift, drop, bias_own, seg):
+    for store in stores:
+        store.wait()
+
+
+def first(nz, tok, joint, mix, lift, drop, biases, seg):
     tokens = tok.shape[0]
     vmem = pl.BlockSpec(memory_space=pltpu.VMEM)
+    hbm = pl.BlockSpec(memory_space=pl.ANY)
     unit = (nz, 2, 2, 2, 16, 512)
     return pl.pallas_call(
         functools.partial(first_kernel, nz),
-        in_specs=[vmem] * 7,
-        out_specs=[vmem] * 6,
+        in_specs=[hbm] + [vmem] * 9,
+        out_specs=[hbm] * 4 + [vmem] * 3,
         out_shape=[
             jax.ShapeDtypeStruct((tokens, 1536), BF),
             jax.ShapeDtypeStruct((3,) + unit, BF),
             jax.ShapeDtypeStruct(unit, BF),
             jax.ShapeDtypeStruct((EARLY,) + unit, BF),
+            jax.ShapeDtypeStruct((drop.shape[0] // 8 - EARLY, 16, 512), BF),
             jax.ShapeDtypeStruct((8, 512), F32),
             jax.ShapeDtypeStruct((seg.shape[0], 128), jnp.int32),
         ],
-        scratch_shapes=[pltpu.VMEM((nz, 2, 2, 2, 16, 128), BF)] + sems(5 + EARLY, nz),
+        scratch_shapes=[
+            pltpu.VMEM(tok.shape, BF),
+            pltpu.VMEM((tokens, 1536), BF),
+            pltpu.VMEM((3,) + unit, BF),
+            pltpu.VMEM(unit, BF),
+            pltpu.VMEM((EARLY,) + unit, BF),
+            pltpu.VMEM((nz, 2, 2, 2, 16, 128), BF),
+            pltpu.VMEM((128, 128), F32),
+            pltpu.SemaphoreType.DMA,
+            pltpu.SemaphoreType.DMA((3,)),
+            pltpu.SemaphoreType.DMA((4 + EARLY,)),
+        ]
+        + sems(5 + EARLY, nz),
         compiler_params=pltpu.CompilerParams(vmem_limit_bytes=VMEM_LIMIT, collective_id=1, has_side_effects=True),
         name="gather_joint",
-    )(tok, joint, mix, lift, drop, bias_own, seg)
+    )(tok, joint, mix, lift, drop, *biases, seg)
 
 
 def middle_kernel(
     nz,
     tb,
-    tok_ref,
-    ctx_ref,
-    cot_ref,
+    tok_hbm,
+    ctx_hbm,
+    cot_hbm,
     mix_ref,
     early_ref,
     late_ref,
     bias_ref,
-    out_ref,
-    gmid_ref,
-    gctx_ref,
+    out_hbm,
+    gmid_hbm,
+    gctx_hbm,
     gmix_ref,
     gbias_ref,
     kept_ref,
     grad_ref,
+    tok_ref,
+    ctx_ref,
+    cot_ref,
+    out_ref,
+    gmid_ref,
+    gctx_ref,
+    in_sem,
+    out_sem,
+    kept_sem,
     w_ref,
     hid_ref,
     hidt_ref,
@@ -724,6 +789,8 @@
     gdt_ref,
     sum_ref,
     load_sem,
+    gsend,
+    grecv,
     rsend,
     rrecv,
     *bufs,
@@ -733,22 +800,38 @@
     nf = w_ref.shape[0] // 2
     nb = tokens // tb
     early = early_ref.shape[0]
-    loads = [pltpu.make_async_copy(early_ref, w_ref.at[0:early], load_sem.at[0])]
+
+    def moves(pairs, sem, b):
+        rows = pl.ds(b * tb, tb)
+        return [pltpu.make_async_copy(x.at[rows], y.at[rows], sem.at[i, b]) for i, (x, y) in enumerate(pairs)]
+
+    ins = ((tok_hbm, tok_ref), (ctx_hbm, ctx_ref), (cot_hbm, cot_ref))
+    outs = ((out_ref, out_hbm), (gmid_ref, gmid_hbm), (gctx_ref, gctx_hbm))
+    for b in range(nb):
+        for move in moves(ins, in_sem, b):
+            move.start()
+    load = pltpu.make_async_copy(early_ref, w_ref.at[0:early], load_sem)
+    load.start()
     for u in range(early, 2 * nf):
-        at = (u - early) * 512
-        loads.append(pltpu.make_async_copy(late_ref.at[:, at : at + 512], w_ref.at[u], load_sem.at[u]))
-    for load in loads:
-        load.start()
+        w_ref[u, me.z, me.y, me.x, me.c] = late_ref[u - early]
     ones = jnp.ones((16, tb), BF)
+
+    late = [Gather(me, w_ref.at[u], gsend, grecv, u - early) for u in range(early, 2 * nf)]
+
+    def gather_step(k):
+        for job in late:
+            (job.start, job.step1, job.step2, job.step3, job.step4)[k]()
 
     def reduces(f):
         return [Reduce(me, bufs, 2 * f + i, rsend, rrecv) for i in range(2)]
 
     me.greet()
-
-    @pl.loop(0, nb)
-    def _(b):
-        rows = pl.ds(pl.multiple_of(b * tb, tb), tb)
+    gather_step(0)
+
+    for b in range(nb):
+        for move in moves(ins, in_sem, b):
+            move.wait()
+        rows = pl.ds(b * tb, tb)
         mid = tok_ref[rows, :].astype(F32) + mm(ctx_ref[rows, :], mix_ref[...]) + bias_ref[5:6, :]
         acc_ref[rows, :] = mid + bias_ref[4:5, :]
         h = mid.astype(BF)
@@ -760,13 +843,12 @@
         gmid_ref[rows, :] = c.astype(F32)
 
     gbias_ref[...] = jnp.zeros_like(gbias_ref)
-    for load in loads:
-        load.wait()
+    load.wait()
 
     def stage1(f, b):
         rows = pl.ds(b * tb, tb)
-        lw = w_ref[2 * f]
-        dw = w_ref[2 * f + 1]
+        lw = w_ref[2 * f].reshape(512, 512)
+        dw = w_ref[2 * f + 1].reshape(512, 512)
         for n in range(0, 512, 256):
             x = mm(hid_ref[rows, :], lw[:, n : n + 256]) + bias_ref[pl.ds(f, 1), n : n + 256]
             grad = mm(cot_ref[rows, :], dw[n : n + 256, :], NT)
@@ -779,8 +861,8 @@
         rows = pl.ds(b * tb, tb)
         act = act_ref[b]
         gl = gl_ref[b]
-        acc_ref[rows, :] += mm(act, w_ref[2 * f + 1])
-        gmid_ref[rows, :] += mm(gl, w_ref[2 * f], NT)
+        acc_ref[rows, :] += mm(act, w_ref[2 * f + 1].reshape(512, 512))
+        gmid_ref[rows, :] += mm(gl, w_ref[2 * f].reshape(512, 512), NT)
         gd = mm(cott_ref[:, rows], act)
         gf = mm(hidt_ref[:, rows], gl)
         unit = gf[:width].reshape(nz, 2, 2, 2, 16, 512)
@@ -795,6 +877,9 @@
             sum_ref[slot, 0] += unit
         gbias_ref[pl.ds(f, 1), :] += gf[width : width + 1]
 
+    def due(k):
+        return [((d - k) // nb, step) for step, d in enumerate(REDUCE_AT) if d % nb == k][::-1]
+
     def reduce_step(f, k):
         slot = f % 2
         for i, job in enumerate(reduces(f)):
@@ -812,32 +897,32 @@
     @pl.loop(0, nf)
     def _(f):
         for k in range(nb):
-
-            @pl.when(f > 0)
-            def _(k=k):
-                if k == 0:
-                    reduce_step(f - 1, 0)
-                if k == 1:
-                    reduce_step(f - 1, 1)
-                if k == 3:
-                    reduce_step(f - 1, 2)
-
-            @pl.when(f > 1)
-            def _(k=k):
-                if k == 1:
-                    reduce_step(f - 2, 3)
-                if k == 3:
-                    reduce_step(f - 2, 4)
+            for at, step in GATHER_AT:
+                if at % nb == k:
+
+                    @pl.when(f == at // nb)
+                    def _(step=step):
+                        gather_step(step)
+
+
+            for back, step in due(k):
+
+                @pl.when(f > back)
+                def _(back=back, step=step):
+                    reduce_step(f - 1 - back, step)
 
             stage1(f, k)
             if k > 0:
                 stage2(f, k - 1)
         stage2(f, nb - 1)
 
+    keep = pltpu.make_async_copy(sum_ref.at[(nf - 1) % 2], kept_ref, kept_sem)
+    keep.start()
     gmix_ref[...] = jnp.zeros_like(gmix_ref)
     for b in range(nb):
-        if b == 1:
-            reduce_step(nf - 2, 3)
+        for back, step in due(b):
+            if back > 0:
+                reduce_step(nf - 1 - back, step)
         rows = pl.ds(b * tb, tb)
         out_ref[rows, :] = acc_ref[rows, :].astype(BF)
         gb = gmid_ref[rows, :].astype(BF)
@@ -845,8 +930,19 @@
         gmix_ref[...] += mm(ctx_ref[rows, :].T, gb)
         gbias_ref[5:6, :] += mm(ones, gb)[0:1]
         gbias_ref[4:5, :] += mm(ones, cot_ref[rows, :])[0:1]
-    kept_ref[...] = sum_ref[(nf - 1) % 2]
-    reduce_step(nf - 2, 4)
+        for move in moves(outs, out_sem, b):
+            move.start()
+    for more in range(1, 4):
+        for b in range(nb):
+            for back, step in due(b):
+                if back > more and nf - 1 - back + more < nf - 1:
+                    reduce_step(nf - 1 - back + more, step)
+    keep.wait()
+    for b in range(nb):
+        for move in moves(outs, out_sem, b):
+            move.wait()
+    for job in late:
+        job.finish()
     for f in range(nf - 1):
         for job in reduces(f):
             job.finish()
@@ -854,13 +950,14 @@
 
 def middle(nz, tok, ctx, cot, mix, early, late, bias):
     tokens, width = tok.shape
-    n = early.shape[0] + late.shape[1] // 512
+    n = early.shape[0] + late.shape[0]
     tb = tokens // 4
     vmem = pl.BlockSpec(memory_space=pltpu.VMEM)
+    hbm = pl.BlockSpec(memory_space=pl.ANY)
     return pl.pallas_call(
         functools.partial(middle_kernel, nz, tb),
-        in_specs=[vmem] * 4 + [pl.BlockSpec(memory_space=pl.ANY)] * 2 + [vmem],
-        out_specs=[vmem] * 7,
+        in_specs=[hbm] * 3 + [vmem, hbm, vmem, vmem],
+        out_specs=[hbm] * 3 + [vmem, vmem, hbm, vmem],
         out_shape=[
             jax.ShapeDtypeStruct((tokens, width), BF),
             jax.ShapeDtypeStruct((tokens, width), F32),
@@ -871,7 +968,16 @@
             jax.ShapeDtypeStruct((n - 2, 16, 512), F32),
         ],
         scratch_shapes=[
-            pltpu.VMEM((n, 512, 512), BF),
+            pltpu.VMEM((tokens, width), BF),
+            pltpu.VMEM((tokens, width), BF),
+            pltpu.VMEM((tokens, width), BF),
+            pltpu.VMEM((tokens, width), BF),
+            pltpu.VMEM((tokens, width), F32),
+            pltpu.VMEM((tokens, width), BF),
+            pltpu.SemaphoreType.DMA((3, 4)),
+            pltpu.SemaphoreType.DMA((3, 4)),
+            pltpu.SemaphoreType.DMA,
+            pltpu.VMEM((n, nz, 2, 2, 2, 16, 512), BF),
             pltpu.VMEM((tokens, width), BF),
             pltpu.VMEM((width + 16, tokens), BF),
             pltpu.VMEM((width, tokens), BF),
@@ -880,8 +986,9 @@
             pltpu.VMEM((4, tb, 512), BF),
             pltpu.VMEM((width, 512), F32),
             pltpu.VMEM((2, 2, nz, 2, 2, 2, 16, 512), F32),
-            pltpu.SemaphoreType.DMA((n,)),
+            pltpu.SemaphoreType.DMA,
         ]
+        + sems(late.shape[0], nz)
         + sems(n - 2, nz)
         + reduce_bufs(n - 2, nz, 512),
         compiler_params=pltpu.CompilerParams(vmem_limit_bytes=VMEM_LIMIT, collective_id=2, has_side_effects=True),
@@ -891,8 +998,8 @@
 
 def last_kernel(
     nz,
-    tok_ref,
-    gj_ref,
+    tok_hbm,
+    gj_hbm,
     gmix_ref,
     gbias_ref,
     kept_ref,
@@ -902,6 +1009,10 @@
     obias_ref,
     glift_ref,
     gdrop_ref,
+    tok_ref,
+    gj_ref,
+    tok_sem,
+    gj_sem,
     tokt_ref,
     sum_ref,
     bsum_ref,
@@ -914,6 +1025,13 @@
 ):
     me = Place(nz)
     tokens, width = tok_ref.shape
+    tok_load = pltpu.make_async_copy(tok_hbm, tok_ref, tok_sem)
+    tok_load.start()
+    gj_loads = []
+    for u in range(3):
+        columns = slice(u * 512, (u + 1) * 512)
+        gj_loads.append(pltpu.make_async_copy(gj_hbm.at[:, columns], gj_ref.at[:, columns], gj_sem.at[u]))
+        gj_loads[u].start()
     n = 7
     nf = glift_ref.shape[1] // 512
     me.greet()
@@ -924,7 +1042,9 @@
         if u == n - 1:
             bsum_ref[...] = brow_ref[...].T.reshape(nz, 2, 2, 2, 16, 128)
         elif u > 2:
+            gj_loads[u - 3].wait()
             if u == 3:
+                tok_load.wait()
 
                 @pl.loop(0, tokens // 512)
                 def _(b):
@@ -975,7 +1095,7 @@
         elif u < n - 1:
             joint_ref[:, (u - 3) * 512 : (u - 2) * 512] = total
         else:
-            obias_ref[...] = total.T
+            obias_ref[...] = jnp.concatenate([total, jnp.zeros((112, 128), F32)], axis=0).T[:8]
 
     def run(u, k):
         if k == 0:
@@ -1000,18 +1120,23 @@
     tokens, width = tok.shape
     n = grads.shape[0] + 2
     vmem = pl.BlockSpec(memory_space=pltpu.VMEM)
+    hbm = pl.BlockSpec(memory_space=pl.ANY)
     return pl.pallas_call(
         functools.partial(last_kernel, nz),
-        in_specs=[vmem] * 6,
+        in_specs=[hbm] * 2 + [vmem] * 4,
         out_specs=[vmem] * 5,
         out_shape=[
             jax.ShapeDtypeStruct((16, 1536), F32),
             jax.ShapeDtypeStruct((16, 512), F32),
-            jax.ShapeDtypeStruct((128, 16), F32),
+            jax.ShapeDtypeStruct((8, 128), F32),
             jax.ShapeDtypeStruct((16, n // 2 * 512), F32),
             jax.ShapeDtypeStruct((n // 2 * 16, 512), F32),
         ],
         scratch_shapes=[
+            pltpu.VMEM((tokens, width), BF),
+            pltpu.VMEM((tokens, 3 * width), BF),
+            pltpu.SemaphoreType.DMA,
+            pltpu.SemaphoreType.DMA((3,)),
             pltpu.VMEM((width + 16, tokens), BF),
             pltpu.VMEM((3, nz, 2, 2, 2, 16, 512), F32),
             pltpu.VMEM((nz, 2, 2, 2, 16, 128), F32),
@@ -1024,6 +1149,37 @@
         compiler_params=pltpu.CompilerParams(vmem_limit_bytes=VMEM_LIMIT, collective_id=3, has_side_effects=True),
         name="joint_grads",
     )(tok, gj, gmix.reshape(nz, 2, 2, 2, 16, 512), gbias, kept, grads)
+
+
+def hand_out_kernel(*refs):
+    half = (len(refs) - 5) // 2
+    bias_ref = refs[half]
+    outs = refs[half + 1 :]
+    for a, b in zip(refs[:half], outs):
+        b[...] = a[...]
+    lift_ref, drop_ref, mix_ref, joint_ref = outs[half:]
+    rows = bias_ref[...]
+    nf = lift_ref.shape[1] // 16
+    lane = lax.broadcasted_iota(jnp.int32, (1, 128), 1)
+    line = rows[0:1]
+    for f in range(1, nf):
+        line = jnp.where(lane // 16 == f, pltpu.roll(rows[f : f + 1], 16 * f, 1), line)
+    lift_ref[...] = line[:, : lift_ref.shape[1]]
+    drop_ref[...] = rows[4:5, 0:16]
+    mix_ref[...] = rows[5:6, 0:16]
+    joint_ref[...] = rows[6:8, 0:16]
+
+
+def hand_out(arrays, bias_rows, nf):
+    vmem = pl.BlockSpec(memory_space=pltpu.VMEM)
+    shapes = [a.shape for a in arrays] + [(1, 16 * nf), (1, 16), (1, 16), (2, 16)]
+    return pl.pallas_call(
+        hand_out_kernel,
+        in_specs=[vmem] * (len(arrays) + 1),
+        out_specs=[vmem] * len(shapes),
+        out_shape=[jax.ShapeDtypeStruct(s, F32) for s in shapes],
+        name="hand_out",
+    )(*arrays, bias_rows)
 
 
 def remote_body(
@@ -1045,20 +1201,14 @@
     n_tok = rows * length
     tok = tokens.reshape(n_tok, width)
     nf = drop_weight.shape[0] // 16
-    bias_own = jnp.concatenate([lift_bias.reshape(nf, 16), drop_bias[None], mix_bias[None], joint_bias])
-    bias_own = jnp.pad(bias_own, ((0, 120), (0, 0))).T
-    lift_own = lift_weight.reshape(16, -1, nf, 16)
-    late = []
-    for f in range(EARLY // 2, nf):
-        late += [lift_own[:, :, f].reshape(16, 512), drop_weight[16 * f : 16 * f + 16]]
-    late = lax.all_gather(jnp.concatenate(late, axis=1), BOTH, axis=0, tiled=True)
-    qkv, joint_w, mix_w, early, bias, starts = first(
-        nz, tok, joint_weight, mix_weight, lift_weight, drop_weight, bias_own, segment_ids
+    biases = (lift_bias[None], drop_bias[None], mix_bias[None], joint_bias)
+    qkv, joint_w, mix_w, early, late, bias, starts = first(
+        nz, tok, joint_weight, mix_weight, lift_weight, drop_weight, biases, segment_ids
     )
     qkv3 = qkv.reshape(rows, length, 3 * width)
     ctx, lse = attend(starts, fill_lengths, segment_ids, qkv3)
     out, gmid, gctx, gmix, gbias, kept, grads = middle(
-        nz, tok, ctx.reshape(n_tok, width), cotangent.reshape(n_tok, width), mix_w.reshape(width, width), early.reshape(EARLY, 512, 512), late, bias
+        nz, tok, ctx.reshape(n_tok, width), cotangent.reshape(n_tok, width), mix_w.reshape(width, width), early, late, bias
     )
     gjoint, token_grad, out = attend_back(
         starts,
@@ -1073,7 +1223,8 @@
         out.reshape(rows, length, width),
     )
     gj, gm, gb, glift, gdrop = last(nz, tok, gjoint.reshape(n_tok, 3 * width), gmix, gbias, kept, grads)
-    return (out, token_grad, gj, gb[6:8], gm, gb[5], glift, gb[:nf].reshape(-1), gdrop, gb[4])
+    gj, gm, glift, gdrop, blift, bdrop, bmix, bjoint = hand_out((gj, gm, glift, gdrop), gb, nf)
+    return (out, token_grad, gj, bjoint, gm, bmix[0], glift, blift[0], gdrop, bdrop[0])
 
 
 BOTH = ("gx", "gy")

time: 229 us -> 202 us (0.88)
  local copies, waits for them, and re-layouts: 16.9 us -> 0 us
  between operations: 14.3 us -> 0.91 us
  Pallas kernels: 194 us -> 198 us
    pallas_call x1, Pallas kernels: 35.6 us -> 43.8 us  [attend_back(): pl.pallas_call(functools.partial(attend_back_kernel, length=length), grid...]
    unnamed x5 -> x0, local copies, waits for them, and re-layouts: 6.79 us -> none
    slice x4 -> x0, local copies, waits for them, and re-layouts: 4.33 us -> none  [the longest x1 1.65 us: remote_body(): lift_own[:, :, f].reshape(16, 512)]
    pallas_call x3 -> x4, Pallas kernels: 136 us -> 133 us  [the longest x1 57.7 us: middle(): pl.pallas_call(functools.partial(middle_kernel, nz, tb), in_specs=[hbm] *...]
    reshape x4 -> x0, local copies, waits for them, and re-layouts: 2.68 us -> none  [the longest x1 1.24 us: remote_body(): lift_own = lift_weight.reshape(16, -1, nf, 16)]
  transfers between devices with their start and end apart: 1 -> 0, of which waited for: 0 -> 0; matrix products, arithmetic and copies ran while one was open for 2% -> 0% of each run, Pallas kernels for 28% -> 0%
where the time goes in v4:
time: 202 us; the launch traced here: 199 us
  Pallas kernels  198 us (98%)
    pallas_call x1, Pallas kernels, middle(): pl.pallas_call(functools.partial(middle_kernel, nz, tb), in_specs=[hbm] *...  57.7 us
    pallas_call x1, Pallas kernels, attend_back(): pl.pallas_call(functools.partial(attend_back_kernel, length=length), grid...  43.8 us
    pallas_call x1, Pallas kernels, last(): pl.pallas_call(functools.partial(last_kernel, nz), in_specs=[hbm] * 2 + [...  36.7 us
    pallas_call x1, Pallas kernels, first(): pl.pallas_call(functools.partial(first_kernel, nz), in_specs=[hbm] + [vme...  36.7 us
    pallas_call x1, Pallas kernels, attend(): pl.pallas_call(functools.partial(attend_kernel, length=length), grid_spec...  21 us

profile of v4, /device:TPU:0, one launch (start us, length us, event | category | flops | bytes accessed | tf_op | source)
XLA Modules:
  0.0 198.6 jit_solution(15253494517394087428)
XLA Ops:
  0.6 36.7 %gather_joint.1 = (bf16[2048,1536]{1,0:T(8,128)(2,1)}, bf16[3,4,2,2,2,16,512]{6,5,4,3,2,1,0:T(8,128)(2,1)}, bf16[4,2,2,2,16,512]{5,4,3,2,1,0:T(8,128)(2,1)}, bf1...) custom-call(bf16[2048,512]{1,0:T(8,128)(2,1)} %bitcast.19, ...), custom_call_target="tpu_custom_call" | custom-call | tf_op jit(solution)/shard_map/gather_joint/pallas_call | solution.py:725
  37.3 21.0 %attend.1 = (bf16[2,1024,512]{2,1,0:T(8,128)(2,1)}, f32[2,4,8,256]{3,2,1,0:T(8,128)}) custom-call(s32[2,128]{1,0:T(2,128)} %get-tuple-element.42.starts_ref, s32[2]{0:T(128)} %fill_ref.3, s32[2,1024]{1,0:T(2,128)} %seg_ref.5, bf16[2,1024,1536]{2,1,0:T(8,128)(2,1)} %bitcast.17), custom_call_target="tpu_custom_call" | custom-call | tf_op jit(solution)/shard_map/attend/pallas_call | solution.py:134
  58.3 57.7 %feed.1 = (bf16[2048,512]{1,0:T(8,128)(2,1)}, f32[2048,512]{1,0:T(8,128)}, bf16[2048,512]{1,0:T(8,128)(2,1)}, f32[512,512]{1,0:T(8,128)}, f32[8,512]{1,0:T(8,128...) custom-call(bf16[2048,512]{1,0:T(8,128)(2,1)} %bitcast.20, bf16[2048,512]{1,0:T(8,128)(2,1)} %bitcast.22, ...), custom_call_target="tpu_custom_call" | custom-call | tf_op jit(solution)/shard_map/feed/pallas_call | solution.py:957
  116.0 43.8 %attend_back.1 = (bf16[2,1024,1536]{2,1,0:T(8,128)(2,1)}, f32[2,1024,512]{2,1,0:T(8,128)}, bf16[2,1024,512]{2,1,0:T(8,128)(2,1)}) custom-call(s32[2,128]{1,0:T(2,128)} %get-tuple-element.42.starts_ref, s32[2]{0:T(128)} %fill_ref.3, s32[2,1024]{1,0:T(2,128)} %seg_ref.5, bf16[2,1024,1536]{2,1,0:T(8,128)(2,1)} %bitcast.18, ...), custom_call_target="tpu_custom_call" | custom-call | tf_op jit(solution)/shard_map/attend_back/pallas_call | solution.py:259
  159.8 36.7 %joint_grads.1 = (f32[16,1536]{1,0:T(8,128)}, f32[16,512]{1,0:T(8,128)}, f32[8,128]{1,0:T(8,128)}, f32[16,2048]{1,0:T(8,128)}, f32[64,512]{1,0:T(8,128)}) custom-call(bf16[2048,512]{1,0:T(8,128)(2,1)} %bitcast.21, bf16[2048,1536]{1,0:T(8,128)(2,1)} %bitcast.23, f32[4,2,2,2,16,512]{5,4,3,2,1,0:T(8,128)} %bitcast.29, f32[8,512]{1,0:T(8,128)} %get-tuple-element.58.gbias_ref, ...), custom_call_target="tpu_custom_call" | custom-call | tf_op jit(solution)/shard_map/joint_grads/pallas_call | solution.py:1124
  196.6 1.8 hand_out.1
